TPU v7x, 32 devices: a whole 2x2x4 slice. The times are simulated.
32 devices in a mesh: dp: 8 (over y, x, core), tensor: 4 (over z).
Axes of the slice: x: 2, y: 2, z: 4, core: 2. Of those that a mesh axis runs over, the one named last changes fastest.
Arguments:
- hidden_in: bfloat16 [8192, 2048], P('dp'), may hold values from -6 to 6
- norm_gain: float32 [2048], replicated, may hold values from 0.5 to 1.5
- z_weight: bfloat16 [2048, 4096], P(None, 'tensor'), may hold values from -0.125 to 0.125
- x_weight: bfloat16 [2048, 4096], P(None, 'tensor'), may hold values from -0.125 to 0.125
- bc_weight: bfloat16 [2048, 256], replicated, may hold values from -0.125 to 0.125
- dt_weight: bfloat16 [2048, 64], P(None, 'tensor'), may hold values from -0.125 to 0.125
- conv_x: float32 [4, 4096], P(None, 'tensor'), may hold values from -3 to 3
- conv_x_bias: float32 [4096], P('tensor'), may hold values from -3 to 3
- conv_bc: float32 [4, 256], replicated, may hold values from -3 to 3
- conv_bc_bias: float32 [256], replicated, may hold values from -3 to 3
- dt_bias: float32 [64], P('tensor'), may hold values from -7 to -3.5
- a_log: float32 [64], P('tensor'), may hold values from 0 to 2.1
- d_skip: float32 [64], P('tensor'), may hold values from 0.3 to 3.5, as said below
- gate_gain: float32 [4096], P('tensor'), may hold values from 0.5 to 1.5
- out_weight: bfloat16 [4096, 2048], P('tensor'), may hold values from -0.09375 to 0.09375
- cotangent: bfloat16 [8192, 2048], P('dp'), may hold values from -6 to 6
- segment_ids: int32 [8192], P('dp'), may hold values from 0 to 31, never falling along the last dimension, each value on 1 to 512 neighbouring positions
Outputs:
- output: float32 [8192, 2048], P('dp')
- input_grad: float32 [8192, 2048], P('dp')
- norm_gain_grad: float32 [2048], replicated
- z_weight_grad: float32 [2048, 4096], P('dp', 'tensor')
- x_weight_grad: float32 [2048, 4096], P('dp', 'tensor')
- bc_weight_grad: float32 [2048, 256], P('dp')
- dt_weight_grad: float32 [2048, 64], P('dp', 'tensor')
- conv_x_grad: float32 [4, 4096], P(None, 'tensor')
- conv_x_bias_grad: float32 [4096], P('tensor')
- conv_bc_grad: float32 [4, 256], replicated
- conv_bc_bias_grad: float32 [256], replicated
- dt_bias_grad: float32 [64], P('tensor')
- a_log_grad: float32 [64], P('tensor')
- d_skip_grad: float32 [64], P('tensor')
- gate_gain_grad: float32 [4096], P('tensor')
- out_weight_grad: float32 [4096, 2048], P('tensor', 'dp')
Inputs may be any that keep to these rules, and one draw needn't show every extreme that they name: `segment_ids`: document numbers never fall along the tokens; a document has at most 512 tokens. `d_skip`: positive.
All inputs are finite; a program needn't handle non-finite values.
Results may differ from a plain program's by a relative error of at most 0.0092.
Values sent between devices are 32-bit elements; how exact they have to be, the bound alone decides.
No kernel may reach another device: no remote copies, remote signals or barrier semaphores. Data moves between devices by JAX's collectives and lax.ppermute only.
A program may use at most 192 MiB of HBM per device.

v0:
```python
from functools import partial

import jax
import jax.numpy as jnp
from jax import lax
from jax.sharding import PartitionSpec as P

D_INNER = 4096
GROUP = 256
SEQ_LEN = 1024


epsilon = 1e-05


def causal_conv(values, kernel_taps, shift_bias, segment_ids, seq_len):
    length = values.shape[0]
    position = jnp.arange(length, dtype=jnp.int32) % seq_len
    result = shift_bias[None, :] + kernel_taps[0][None, :] * values
    for offset in range(1, kernel_taps.shape[0]):
        shifted = jnp.concatenate(
            [jnp.zeros((offset, values.shape[1]), values.dtype), values[:-offset]], 0
        )
        shifted_ids = jnp.concatenate(
            [jnp.full((offset,), -1, jnp.int32), segment_ids[:-offset]], 0
        )
        usable = (position >= offset) & (shifted_ids == segment_ids)
        result = result + jnp.where(usable[:, None], shifted, 0.0) * kernel_taps[offset][None, :]
    return result


def block_scan(inputs_x, steps_dt, rates, b_rows, c_rows, segment_ids, seq_len):
    length, head_count, head_width = inputs_x.shape
    states_n = b_rows.shape[1]
    blocks = length // GROUP
    per_sequence = seq_len // GROUP
    decays = steps_dt * rates[None, :]

    def to_blocks(source):
        return source.reshape((blocks, GROUP) + source.shape[1:])

    def advance(carried, pieces):
        memory, last_id = carried
        block_x, block_dt, block_decay, block_b, block_c, block_ids, number = pieces
        is_fresh = number % per_sequence == 0
        running = jnp.cumsum(block_decay, axis=0)
        across = running.T
        gap_matrix = across[:, :, None] - across[:, None, :]
        lower_mask = jnp.arange(GROUP)[:, None] >= jnp.arange(GROUP)[None, :]
        linked = (lower_mask & (block_ids[:, None] == block_ids[None, :]))[None]
        factors = jnp.where(linked, jnp.exp(jnp.where(linked, gap_matrix, 0.0)), 0.0)
        scores = jnp.dot(block_c, block_b.T, precision=lax.Precision.HIGHEST)
        weighted = scores[None] * factors * block_dt.T[:, None, :]
        inside = jnp.einsum("hts,shp->thp", weighted, block_x, precision=lax.Precision.HIGHEST)
        reading = jnp.logical_and(block_ids == last_id, jnp.logical_not(is_fresh))
        reach = jnp.exp(running) * jnp.where(reading, 1.0, 0.0)[:, None]
        outside = (
            jnp.einsum("tn,hnp->thp", block_c, memory, precision=lax.Precision.HIGHEST)
            * reach[:, :, None]
        )
        final_id = block_ids[-1]
        keeping = jnp.where(
            jnp.logical_and(final_id == last_id, jnp.logical_not(is_fresh)), 1.0, 0.0
        )
        tail_weights = (
            jnp.exp(running[-1][None, :] - running)
            * block_dt
            * jnp.where(block_ids == final_id, 1.0, 0.0)[:, None]
        )
        memory = keeping * jnp.exp(running[-1])[:, None, None] * memory + jnp.einsum(
            "sn,shp->hnp",
            block_b,
            tail_weights[:, :, None] * block_x,
            precision=lax.Precision.HIGHEST,
        )
        return ((memory, final_id), inside + outside)

    initial = (
        jnp.zeros((head_count, states_n, head_width), inputs_x.dtype),
        jnp.array(-1, jnp.int32),
    )
    numbers = jnp.arange(blocks, dtype=jnp.int32)
    final_carry, outputs = lax.scan(
        jax.checkpoint(advance),
        initial,
        (
            to_blocks(inputs_x),
            to_blocks(steps_dt),
            to_blocks(decays),
            to_blocks(b_rows),
            to_blocks(c_rows),
            to_blocks(segment_ids),
            numbers,
        ),
    )
    return outputs.reshape(length, head_count, head_width)


def bc_branch(segment_ids, seq_len, bc_pre, conv_bc, conv_bc_bias):
    return jax.nn.silu(causal_conv(bc_pre, conv_bc, conv_bc_bias, segment_ids, seq_len))


def mixer_tail(
    segment_ids, seq_len, x_pre, bc_conv, dt_pre, z_pre, conv_x, conv_x_bias, dt_bias, a_log, d_skip
):
    length = x_pre.shape[0]
    head_count = dt_pre.shape[1]
    x_conv = jax.nn.silu(causal_conv(x_pre, conv_x, conv_x_bias, segment_ids, seq_len))
    states_n = bc_conv.shape[1] // 2
    step_sizes = jax.nn.softplus(dt_pre + dt_bias[None, :])
    per_head = x_conv.reshape(length, head_count, -1)
    scanned = block_scan(
        per_head,
        step_sizes,
        -jnp.exp(a_log),
        bc_conv[:, :states_n],
        bc_conv[:, states_n:],
        segment_ids,
        seq_len,
    )
    scanned = scanned + d_skip[None, :, None] * per_head
    return scanned.reshape(length, -1) * jax.nn.silu(z_pre)


def contract_rows(left, right):
    return lax.dot_general(
        left, right, (((0,), (0,)), ((), ())), preferred_element_type=jnp.float32
    )


def contract_cols(left, right):
    return lax.dot_general(
        left, right, (((1,), (1,)), ((), ())), preferred_element_type=jnp.float32
    )


def shards(
    hidden_in,
    norm_gain,
    z_weight,
    x_weight,
    bc_weight,
    dt_weight,
    conv_x,
    conv_x_bias,
    conv_bc,
    conv_bc_bias,
    dt_bias,
    a_log,
    d_skip,
    gate_gain,
    out_weight,
    cotangent,
    segment_ids,
):
    base = hidden_in.astype(jnp.float32)
    rms_inv = lax.rsqrt(jnp.mean(base * base, -1, keepdims=True) + epsilon)
    hat_rows = base * rms_inv
    normed = (hat_rows * norm_gain[None, :]).astype(jnp.bfloat16)
    z_pre = jnp.dot(normed, z_weight, preferred_element_type=jnp.float32)
    x_pre = jnp.dot(normed, x_weight, preferred_element_type=jnp.float32)
    bc_pre = jnp.dot(normed, bc_weight, preferred_element_type=jnp.float32)
    dt_pre = jnp.dot(normed, dt_weight, preferred_element_type=jnp.float32)
    bc_conv, bc_back = jax.vjp(
        partial(bc_branch, segment_ids, SEQ_LEN), bc_pre, conv_bc, conv_bc_bias
    )
    local_mixer = partial(mixer_tail, segment_ids, SEQ_LEN)
    gated, mixer_back = jax.vjp(
        local_mixer, x_pre, bc_conv, dt_pre, z_pre, conv_x, conv_x_bias, dt_bias, a_log, d_skip
    )
    squares = jnp.sum(gated * gated, -1)
    unit = (gated * gate_gain[None, :]).astype(jnp.bfloat16)
    total_sq = lax.psum(squares, "tensor")
    proj = lax.psum(jnp.dot(unit, out_weight, preferred_element_type=jnp.float32), "tensor")
    scale = lax.rsqrt(total_sq / D_INNER + epsilon)[:, None]
    output = base + scale * proj
    cot_rows = cotangent.astype(jnp.float32)
    d_scale = jnp.sum(cot_rows * proj, -1, keepdims=True)
    d_proj = (scale * cot_rows).astype(jnp.bfloat16)
    out_grad_full = contract_rows(unit, d_proj)
    d_unit = contract_cols(d_proj, out_weight)
    gate_grad_local = jnp.sum(d_unit * gated, 0)
    d_gated = d_unit * gate_gain[None, :] - d_scale * scale * scale * scale * gated / D_INNER
    (
        d_x,
        d_bc_conv_part,
        d_dt,
        d_z,
        conv_x_local,
        conv_x_bias_local,
        dt_bias_local,
        a_log_local,
        d_skip_local,
    ) = mixer_back(d_gated)
    d_z_low = d_z.astype(jnp.bfloat16)
    d_x_low = d_x.astype(jnp.bfloat16)
    d_dt_low = d_dt.astype(jnp.bfloat16)
    normed_part = (
        contract_cols(d_z_low, z_weight)
        + contract_cols(d_x_low, x_weight)
        + contract_cols(d_dt_low, dt_weight)
    )
    d_normed_sum, d_bc_conv_full = lax.psum((normed_part, d_bc_conv_part), "tensor")
    d_bc_full, conv_bc_full, conv_bc_bias_full = bc_back(d_bc_conv_full)
    d_bc_low = d_bc_full.astype(jnp.bfloat16)
    d_normed = d_normed_sum + contract_cols(d_bc_low, bc_weight)
    z_grad_full = contract_rows(normed, d_z_low)
    x_grad_full = contract_rows(normed, d_x_low)
    bc_grad_full = contract_rows(normed, d_bc_low)
    dt_grad_full = contract_rows(normed, d_dt_low)
    norm_grad_local = jnp.sum(d_normed * hat_rows, 0)
    d_hat = d_normed * norm_gain[None, :]
    input_grad = cot_rows + rms_inv * (
        d_hat - hat_rows * jnp.mean(d_hat * hat_rows, -1, keepdims=True)
    )
    z_share, x_share, bc_share, dt_share, out_share = (
        lax.psum_scatter(z_grad_full, "dp", scatter_dimension=0, tiled=True),
        lax.psum_scatter(x_grad_full, "dp", scatter_dimension=0, tiled=True),
        lax.psum_scatter(bc_grad_full, "dp", scatter_dimension=0, tiled=True),
        lax.psum_scatter(dt_grad_full, "dp", scatter_dimension=0, tiled=True),
        lax.psum_scatter(out_grad_full, "dp", scatter_dimension=1, tiled=True),
    )
    (
        norm_gain_grad,
        conv_x_grad,
        conv_x_bias_grad,
        conv_bc_grad,
        conv_bc_bias_grad,
        dt_bias_grad,
        a_log_grad,
        d_skip_grad,
        gate_gain_grad,
    ) = lax.psum(
        (
            norm_grad_local,
            conv_x_local,
            conv_x_bias_local,
            conv_bc_full,
            conv_bc_bias_full,
            dt_bias_local,
            a_log_local,
            d_skip_local,
            gate_grad_local,
        ),
        "dp",
    )
    return (
        output,
        input_grad,
        norm_gain_grad,
        z_share,
        x_share,
        bc_share,
        dt_share,
        conv_x_grad,
        conv_x_bias_grad,
        conv_bc_grad,
        conv_bc_bias_grad,
        dt_bias_grad,
        a_log_grad,
        d_skip_grad,
        gate_gain_grad,
        out_share,
    )


def solution(mesh):
    placed = (
        P("dp", None),
        P(),
        P(None, "tensor"),
        P(None, "tensor"),
        P(),
        P(None, "tensor"),
        P(None, "tensor"),
        P("tensor"),
        P(),
        P(),
        P("tensor"),
        P("tensor"),
        P("tensor"),
        P("tensor"),
        P("tensor", None),
        P("dp", None),
        P("dp"),
    )
    return jax.shard_map(
        shards,
        mesh=mesh,
        in_specs=placed,
        out_specs=(
            P("dp", None),
            P("dp", None),
            P(),
            P("dp", "tensor"),
            P("dp", "tensor"),
            P("dp", None),
            P("dp", "tensor"),
            P(None, "tensor"),
            P("tensor"),
            P(),
            P(),
            P("tensor"),
            P("tensor"),
            P("tensor"),
            P("tensor"),
            P("tensor", "dp"),
        ),
        check_vma=False,
    )
```

profile of v0, /device:TPU:0, one launch (start us, length us, event | category | flops | bytes accessed | tf_op | source)
XLA Modules:
  0.0 1425.3 jit_solution(9388116246449049603)
XLA Ops:
  30.1 7.2 reshape.566
  37.3 7.7 copy.113
  52.3 99.0 %while.47 = (s32[]{:T(128)}, f32[16,128,64]{1,2,0:T(8,128)S(1)}, s32[]{:T(128)}, f32[4,256,16,64]{1,3,2,0:T(8,128)}, f32[4,16,128,64]{2,3,1,0:T(8,128)}, /*index...) while((s32[]{:T(128)}, f32[16,128,64]{1,2,0:T(8,128)S(1)}, ...), condition=%wide.region_4.5_spmd.clone, body=%wide.region_1.4_spmd.clone.sunk | while | flops 1718441344 | bytes 9877865 | solution.py:83
  151.3 8.1 copy.125
  159.4 8.1 reshape.563
  167.6 13.2 multiply_reduce_fusion.11
  191.5 13.7 psum.91
  205.2 278.1 %all-reduce.31.cloned.1.call-done = f32[1024,2048]{1,0:T(8,128)} async-done(((f32[1024,2048]{1,0:T(8,128)}), f32[1024,2048]{1,0:T(8,128)}) %all-reduce.31.cloned.1.call-update) | async-done | bytes 8388624 | tf_op jit(solution)/shard_map/psum | solution.py:174
  483.3 10.1 fusion.113
  495.8 13.8 multiply_reduce_fusion.6
  509.7 7.2 reshape.564
  516.9 7.7 copy.120
  530.5 196.7 %while.48 = (s32[]{:T(128)}, f32[16,128,64]{1,2,0:T(8,128)}, f32[4,256,16,64]{1,3,2,0:T(8,128)}, f32[4,256,16]{1,0,2:T(4,128)}, f32[4,256,16]{1,0,2:T(4,128)}, /...) while((s32[]{:T(128)}, f32[16,128,64]{1,2,0:T(8,128)}, ...), condition=%wide.region_22.23_spmd.clone, body=%wide.region_9.22_spmd.clone.sunk | while | flops 3951183104 | bytes 32404336 | solution.py:83
  551.1 8.2 fusion.282
  600.4 8.2 fusion.282
  649.7 8.2 fusion.282
  699.1 8.2 fusion.282
  728.9 8.1 copy.128
  737.0 7.6 reshape.565
  744.7 13.8 fusion.152
  768.1 7.6 fusion.167
  789.9 12.2 fusion.124
  802.2 308.6 %all-reduce.33.cloned.1.call-done = (f32[1024,2048]{1,0:T(8,128)}, f32[1024,256]{1,0:T(8,128)}) async-done(((f32[1024,2048]{1,0:T(8,128)}, f32[1024,256]{1,0:T(8,128)}), (f32[1024,2048]{1,0:T(8,128)}, f32[1024,256]{1,0:T(8,128)})) %all-reduce.33.cloned.1.call-update) | async-done | bytes 9437200 | tf_op jit(solution)/shard_map/psum | solution.py:203
  1119.5 9.1 fusion.169
  1130.2 9.0 fusion.168
  1140.3 8.1 fusion.110
  1148.4 25.0 %all-reduce.26 = (f32[2048]{0:T(1024)}, f32[4,1024]{1,0:T(4,128)}, f32[1024]{0:T(1024)}, f32[4,256]{1,0:T(4,128)}, f32[256]{0:T(256)}, /*index=5*/f32[16]{0:T(128)}, f32[16]{0:T(128)}, f32[16]{0:T(128)}, f32[1024]{0:T(1024)}) all-reduce(f32[2048]{0:T(1024)S(1)} %get-tuple-element.842, ...), channel_id=1, replica_groups=mesh['dp'=8,'tensor'=4] {'dp'}, use_global_device_ids=true, to_apply=%region_27.28 | all-reduce | flops 9520 | bytes 76160 | tf_op jit(solution)/shard_map/psum | solution.py:233
  1173.4 10.5 convert_add_fusion
  1183.9 38.5 %reduce-scatter.14.cloned.1.call-done = f32[1024,256]{1,0:T(8,128)} async-done(((f32[1024,2048]{1,0:T(8,128)}), f32[1024,256]{1,0:T(8,128)}) %reduce-scatter.14.cloned.1.call-update) | async-done | bytes 1048592 | tf_op jit(solution)/shard_map/reduce_scatter | solution.py:221
  1222.4 44.9 %reduce-scatter.10.cloned.1.call-done = f32[256,256]{1,0:T(8,128)} async-done(((f32[2048,256]{1,0:T(8,128)}), f32[256,256]{1,0:T(8,128)}) %reduce-scatter.10.cloned.1.call-update) | async-done | bytes 262160 | tf_op jit(solution)/shard_map/reduce_scatter | solution.py:219
  1267.3 75.6 %reduce-scatter.8.cloned.1.call-done = f32[256,1024]{1,0:T(8,128)} async-done(((f32[2048,1024]{1,0:T(8,128)}), f32[256,1024]{1,0:T(8,128)}) %reduce-scatter.8.cloned.1.call-update) | async-done | bytes 1048592 | tf_op jit(solution)/shard_map/reduce_scatter | solution.py:218
  1343.0 75.3 %reduce-scatter.6.cloned.1.call-done = f32[256,1024]{1,0:T(8,128)} async-done(((f32[2048,1024]{1,0:T(8,128)}), f32[256,1024]{1,0:T(8,128)}) %reduce-scatter.6.cloned.1.call-update) | async-done | bytes 1048592 | tf_op jit(solution)/shard_map/reduce_scatter | solution.py:217
  (501 shorter events, 320.5 us)
Async XLA Ops:
  7.2 476.1 %all-reduce.31.cloned.1.call-start = ((), (), s32[]{:S(2)}) async-start(), calls=%async_computation.5 | async-start | bytes 16777216 | tf_op jit(solution)/shard_map/psum | solution.py:174
  15.8 173.9 %copy-start.28 = (pred[1024]{0:T(1024)(128)(4,1)}, pred[1024]{0:T(1024)(128)(4,1)S(1)}, u32[]{:S(2)}) copy-start(pred[1024]{0:T(1024)(128)(4,1)S(1)} %get-tuple-element.981) | copy-start | bytes 3076
  15.8 174.5 %copy-start.30 = (pred[1024]{0:T(1024)(128)(4,1)}, pred[1024]{0:T(1024)(128)(4,1)S(1)}, u32[]{:S(2)}) copy-start(pred[1024]{0:T(1024)(128)(4,1)S(1)} %get-tuple-element.982) | copy-start | bytes 3076
  15.8 175.1 %copy-start.26 = (pred[1024]{0:T(1024)(128)(4,1)}, pred[1024]{0:T(1024)(128)(4,1)S(1)}, u32[]{:S(2)}) copy-start(pred[1024]{0:T(1024)(128)(4,1)S(1)} %get-tuple-element.980) | copy-start | bytes 3076
  167.6 325.9 %copy-start.43 = (f32[1024]{0:T(1024)}, f32[1024]{0:T(1024)S(1)}, u32[]{:S(2)}) copy-start(f32[1024]{0:T(1024)S(1)} %mul.920) | copy-start | bytes 12292
  167.6 15.2 %copy-start.65 = (bf16[1024,2048]{1,0:T(8,128)(2,1)S(1)}, bf16[1024,2048]{1,0:T(8,128)(2,1)}, u32[]{:S(2)}) copy-start(bf16[1024,2048]{1,0:T(8,128)(2,1)} %param.35) | copy-start | bytes 12582916
  167.6 15.2 %copy-start.68 = (f32[1024]{0:T(1024)S(1)}, f32[1024]{0:T(1024)}, u32[]{:S(2)}) copy-start(f32[1024]{0:T(1024)} %param.34) | copy-start | bytes 12292
  189.6 921.3 %all-reduce.33.cloned.1.call-start = ((), (), s32[]{:S(2)}) async-start(), calls=%async_computation.11 | async-start | bytes 18874368 | tf_op jit(solution)/shard_map/psum | solution.py:203
  205.2 288.3 %copy-start.40 = (f32[1024]{0:T(1024)}, f32[1024]{0:T(1024)S(1)}, u32[]{:S(2)}) copy-start(f32[1024]{0:T(1024)S(1)} %add_rsqrt_fusion) | copy-start | bytes 12292
  483.3 10.2 copy-start.7
  483.3 11.3 copy-start.8
  483.3 12.5 copy-start.10
  550.9 8.4 copy-start.9
  551.1 11.2 copy-start.2
  600.3 8.4 copy-start.9
  600.4 11.2 copy-start.2
  649.6 8.4 copy-start.9
  649.7 8.3 copy-start.17
  649.7 11.2 copy-start.2
  698.9 8.4 copy-start.9
  699.0 8.3 copy-start.17
  699.1 11.2 copy-start.2
  744.7 13.9 copy-start.39
  744.7 13.9 copy-start.47
  786.3 397.6 %reduce-scatter.12.cloned.1.call-start = ((), (), s32[]{:S(2)}) async-start(), calls=%async_computation.9 | async-start | bytes 147456 | tf_op jit(solution)/shard_map/reduce_scatter | solution.py:220
  789.9 432.5 %reduce-scatter.14.cloned.1.call-start = ((), (), s32[]{:S(2)}) async-start(), calls=%async_computation.10 | async-start | bytes 9437184 | tf_op jit(solution)/shard_map/reduce_scatter | solution.py:221
  802.1 308.7 %copy-start.4 = (f32[1024,256]{1,0:T(8,128)S(1)}, f32[1024,256]{1,0:T(8,128)}, u32[]{:S(2)}) copy-start(f32[1024,256]{1,0:T(8,128)} %copy-done.3) | copy-start | bytes 3145732
  802.1 308.7 %copy-start.11 = (f32[1024,256]{1,0:T(8,128)S(1)}, f32[1024,256]{1,0:T(8,128)}, u32[]{:S(2)}) copy-start(f32[1024,256]{1,0:T(8,128)} %get-tuple-element.936) | copy-start | bytes 3145732
  802.2 312.0 %copy-start.53 = (f32[1,256]{1,0:T(1,128)S(1)}, f32[1,256]{1,0:T(1,128)}, u32[]{:S(2)}) copy-start(f32[1,256]{1,0:T(1,128)} %copy-done.52) | copy-start | bytes 3076
  802.2 465.1 %reduce-scatter.10.cloned.1.call-start = ((), (), s32[]{:S(2)}) async-start(), calls=%async_computation.8 | async-start | bytes 2359296 | tf_op jit(solution)/shard_map/reduce_scatter | solution.py:219
  1119.5 223.5 %reduce-scatter.8.cloned.1.call-start = ((), (), s32[]{:S(2)}) async-start(), calls=%async_computation.7 | async-start | bytes 9437184 | tf_op jit(solution)/shard_map/reduce_scatter | solution.py:218
  1128.6 289.6 %reduce-scatter.6.cloned.1.call-start = ((), (), s32[]{:S(2)}) async-start(), calls=%async_computation.6 | async-start | bytes 9437184 | tf_op jit(solution)/shard_map/reduce_scatter | solution.py:217
  (59 other events, 265.2 us)
Sparse Core Ops, SparseCore 0:
  189.7 293.5 all-reduce.30
  786.4 324.3 all-reduce.32
  1114.4 32.3 reduce-scatter.11
  1151.1 71.2 reduce-scatter.13
  1226.1 41.1 reduce-scatter.9
  1271.6 71.3 reduce-scatter.7
  1347.0 71.2 reduce-scatter.5
where the time goes:
time: 1440 us; the launch traced here: 1430 us
  waiting for transfers between devices  821 us (57%)
  matrix products  261 us (18%)
  local copies, waits for them, and re-layouts  159 us (11%)
  other arithmetic  102 us (7%)
  blocking collectives  38.7 us (3%)
  loops' own time  27.7 us (2%)
  between operations  15.2 us (1%)
    psum x1, waiting for transfers between devices, shards(): lax.psum((normed_part, d_bc_conv_part), 'tensor')  309 us
    psum x1, waiting for transfers between devices, shards(): lax.psum(jnp.dot(unit, out_weight, preferred_element_type=jnp.float32), '...  278 us
    dot_general x12, matrix products, advance(): jnp.einsum('hts,shp->thp', weighted, block_x, precision=lax.Precision.HIG...  85.5 us
    reduce_scatter x1, waiting for transfers between devices, shards(): lax.psum_scatter(x_grad_full, 'dp', scatter_dimension=0, tiled=True)  75.6 us
    reduce_scatter x1, waiting for transfers between devices, shards(): lax.psum_scatter(z_grad_full, 'dp', scatter_dimension=0, tiled=True)  75.3 us
    reduce_scatter x1, waiting for transfers between devices, shards(): lax.psum_scatter(bc_grad_full, 'dp', scatter_dimension=0, tiled=True)  44.9 us
    dot_general x5, matrix products, contract_cols(): lax.dot_general(left, right, (((1,), (1,)), ((), ())), preferred_element_...  38.7 us
    reduce_scatter x1, waiting for transfers between devices, shards(): lax.psum_scatter(out_grad_full, 'dp', scatter_dimension=1, tiled=True)  38.5 us
  transfers between devices with their start and end apart: 7, of which 6 were waited for; matrix products, arithmetic and copies ran while one was open for 4% of the time, Pallas kernels for 0%

commit v1 on v0

v1 whole, which is shorter than its diff:
```python
from functools import partial

import jax
import jax.numpy as jnp
from jax import lax
from jax.experimental import pallas as pl
from jax.experimental.pallas import tpu as pltpu
from jax.sharding import PartitionSpec as P

D_INNER = 4096
SEQ_LEN = 1024
CHUNK = 128
HEAD = 64
STATE = 128
PAIR = 2 * HEAD

epsilon = 1e-05

bf16 = jnp.bfloat16
f32 = jnp.float32


def dot(left, right, dims=((1,), (0,))):
    return lax.dot_general(left, right, (dims, ((), ())), preferred_element_type=f32)


def dot_exact(left, right, dims=((1,), (0,))):
    return lax.dot_general(
        left, right, (dims, ((), ())), precision=lax.Precision.HIGHEST, preferred_element_type=f32
    )


def split_dot(values, ones):
    high = values.astype(bf16)
    low = (values - high.astype(f32)).astype(bf16)
    return dot(high, ones) + dot(low, ones)


def sigmoid(v):
    return 1.0 / (1.0 + jnp.exp(-v))


def softplus(v):
    return jnp.maximum(v, 0.0) + jnp.log(1.0 + jnp.exp(-jnp.abs(v)))


PASSES = {q: 3 for q in ("scores", "inside", "outside", "state", "d_weight", "du_tail", "d_b", "d_c", "d_state", "d_scores")}
STATE_TYPE = f32


def two_parts(values):
    high = values.astype(bf16)
    return high, (values - high.astype(f32)).astype(bf16)


def mm(kind, left, right, dims=((1,), (0,))):
    if PASSES.get(kind, 1) == 1:
        return dot(left.astype(bf16), right.astype(bf16), dims)
    left_high, left_low = two_parts(left)
    right_high, right_low = two_parts(right)
    return (
        dot(left_high, right_high, dims)
        + dot(left_high, right_low, dims)
        + dot(left_low, right_high, dims)
    )


def seen(kind, values):
    return values.astype(bf16).astype(f32) if PASSES.get(kind, 1) == 1 else values


def conv_rows(padded, lanes, taps, aux):
    result = taps[4:5] + taps[0:1] * padded[pl.ds(8, CHUNK), lanes]
    for offset in range(1, 4):
        shifted = padded[pl.ds(8 - offset, CHUNK), lanes] * aux[:, offset - 1 : offset]
        result = result + shifted * taps[offset : offset + 1]
    return result


def chunk_terms(dt_ref, aux, head_ref, spread_ref):
    row = lax.broadcasted_iota(jnp.int32, (CHUNK, CHUNK), 0)
    col = lax.broadcasted_iota(jnp.int32, (CHUNK, CHUNK), 1)
    lower = jnp.where(row >= col, 1.0, 0.0)
    upper = jnp.where(row <= col, 1.0, 0.0)
    raw = dt_ref[...] + head_ref[0:1, :]
    step = softplus(raw)
    decay = step * head_ref[1:2, :]
    running = dot_exact(lower, decay)
    running_t = dot_exact(decay, upper, ((0,), (0,)))
    last = running[CHUNK - 1 : CHUNK, :]
    reach = jnp.exp(running) * aux[:, 6:7]
    tail = jnp.exp(last - running) * aux[:, 7:8]
    kept = jnp.exp(last) * aux[CHUNK - 1 : CHUNK, 8:9]
    spread = spread_ref[...]
    return (
        raw,
        step,
        decay,
        running,
        running_t,
        upper,
        split_dot(step, spread),
        split_dot(reach, spread),
        split_dot(tail, spread),
        split_dot(jnp.broadcast_to(kept, (8, kept.shape[1])), spread)[0:1],
    )


def pair_masks():
    lane = lax.broadcasted_iota(jnp.int32, (1, PAIR), 1)
    return jnp.where(lane < HEAD, 1.0, 0.0), jnp.where(lane < HEAD, 0.0, 1.0)


def forward_kernel(
    x_ref, x_before, z_ref, bc_ref, bc_before, dt_ref, aux_ref, ids_ref,
    chan_ref, taps_bc_ref, head_ref, spread_ref, start_ref,
    y_ref, unit_ref, square_ref, states_ref, final_ref,
    x_pad, bc_pad, memory, step_s, reach_s, tail_s,
):
    @pl.when(pl.program_id(0) == 0)
    def _():
        memory[...] = start_ref[...]
        x_pad[0:8, :] = x_before[...]
        bc_pad[0:8, :] = bc_before[...]

    @pl.when(pl.program_id(0) > 0)
    def _():
        x_pad[0:8, :] = x_pad[CHUNK:, :]
        bc_pad[0:8, :] = bc_pad[CHUNK:, :]

    aux = aux_ref[...]
    x_pad[8:, :] = x_ref[...]
    bc_pad[8:, :] = bc_ref[...]
    pre_bc = conv_rows(bc_pad, slice(None), taps_bc_ref[...], aux)
    bc = pre_bc * sigmoid(pre_bc)
    b_rows, c_rows = bc[:, :STATE], bc[:, STATE:]
    _, _, _, running, running_t, _, step_e, reach_e, tail_e, kept_e = chunk_terms(
        dt_ref, aux, head_ref, spread_ref
    )
    step_s[...] = step_e
    reach_s[...] = reach_e
    tail_s[...] = tail_e
    row = lax.broadcasted_iota(jnp.int32, (CHUNK, CHUNK), 0)
    col = lax.broadcasted_iota(jnp.int32, (CHUNK, CHUNK), 1)
    linked = (row >= col) & (aux[:, 9:10] == ids_ref[...])
    scores = jnp.where(linked, mm("scores", c_rows, b_rows, ((1,), (1,))), 0.0)
    first, second = pair_masks()
    squares = jnp.zeros((CHUNK, 1), f32)
    for pair in range(x_ref.shape[1] // PAIR):
        lanes = slice(pair * PAIR, (pair + 1) * PAIR)
        chan = chan_ref[:, lanes]
        pre = conv_rows(x_pad, lanes, chan, aux)
        x_conv = pre * sigmoid(pre)
        u = step_s[:, lanes] * x_conv
        old = memory[:, lanes]
        states_ref[0, :, lanes] = old.astype(states_ref.dtype)
        weighted = []
        for h in (2 * pair, 2 * pair + 1):
            gap = jnp.minimum(running[:, h : h + 1] - running_t[h : h + 1, :], 0.0)
            weighted.append(scores * jnp.exp(gap))
        y = mm(
            "inside", jnp.concatenate(weighted, 1), jnp.concatenate([u * first, u * second], 0)
        ) + mm("outside", c_rows, old) * reach_s[:, lanes]
        memory[:, lanes] = kept_e[:, lanes] * old + mm(
            "state", b_rows, tail_s[:, lanes] * u, ((0,), (0,))
        )
        y_ref[:, lanes] = y
        z = z_ref[:, lanes]
        gated = (y + chan[5:6] * x_conv) * (z * sigmoid(z))
        unit_ref[:, lanes] = (gated * chan[6:7]).astype(bf16)
        squares = squares + jnp.sum(gated * gated, 1, keepdims=True)
    square_ref[...] = squares
    final_ref[...] = memory[...]


def backward_kernel(
    x_ref, x_before, z_ref, bc_ref, bc_before, dt_ref, aux_ref, ids_ref,
    chan_ref, taps_bc_ref, head_ref, spread_ref,
    x_within, bc_within, gather_ref, y_ref, state_ref, next_ref, d_unit_ref, coef_ref,
    d_memory_in, dconv_in, dconv_bc_in, g_chan_in, g_bc_in, g_head_in,
    dz_ref, dx_ref, dbc_ref, ddt_ref,
    d_memory, dconv_ref, dconv_bc_ref, g_chan_ref, g_bc_ref, g_head_ref,
    x_pad, bc_pad, step_s, reach_s, tail_s, dconv_pad, dconv_bc_pad, step_grad_s, run_grad_s, later,
):
    heads = head_ref.shape[1]
    index, count = pl.program_id(0), pl.num_programs(0)

    @pl.when(index == 0)
    def _():
        d_memory[...] = d_memory_in[...]
        dconv_pad[0:8, :] = dconv_in[...]
        dconv_bc_pad[0:8, :] = dconv_bc_in[...]
        g_chan_ref[...] = g_chan_in[...]
        g_bc_ref[...] = g_bc_in[...]
        g_head_ref[...] = g_head_in[...]
        later[...] = next_ref[0]

    @pl.when(index == count - 1)
    def _():
        x_pad[0:8, :] = x_before[...]
        bc_pad[0:8, :] = bc_before[...]

    @pl.when(index < count - 1)
    def _():
        x_pad[0:8, :] = x_within[...]
        bc_pad[0:8, :] = bc_within[...]

    aux = aux_ref[...]
    x_pad[8:, :] = x_ref[...]
    bc_pad[8:, :] = bc_ref[...]
    dconv_pad[CHUNK:, :] = dconv_pad[0:8, :]
    dconv_bc_pad[CHUNK:, :] = dconv_bc_pad[0:8, :]
    taps_bc = taps_bc_ref[...]
    pre_bc = conv_rows(bc_pad, slice(None), taps_bc, aux)
    sig_bc = sigmoid(pre_bc)
    bc = pre_bc * sig_bc
    b_rows, c_rows = bc[:, :STATE], bc[:, STATE:]
    raw, step, decay, running, running_t, upper, step_e, reach_e, tail_e, kept_e = chunk_terms(
        dt_ref, aux, head_ref, spread_ref
    )
    step_s[...] = step_e
    reach_s[...] = reach_e
    tail_s[...] = tail_e
    row = lax.broadcasted_iota(jnp.int32, (CHUNK, CHUNK), 0)
    col = lax.broadcasted_iota(jnp.int32, (CHUNK, CHUNK), 1)
    linked = (row <= col) & (aux[:, 9:10] == ids_ref[...])
    scores_t = jnp.where(linked, mm("scores", b_rows, c_rows, ((1,), (1,))), 0.0)
    first, second = pair_masks()
    coef = coef_ref[...]
    d_scores_t = jnp.zeros((CHUNK, CHUNK), f32)
    d_b = jnp.zeros((CHUNK, STATE), f32)
    d_c = jnp.zeros((CHUNK, STATE), f32)
    ends = jnp.zeros((8, heads), f32)
    for pair in range(x_ref.shape[1] // PAIR):
        lanes = slice(pair * PAIR, (pair + 1) * PAIR)
        chan = chan_ref[:, lanes]
        pre = conv_rows(x_pad, lanes, chan, aux)
        sig = sigmoid(pre)
        x_conv = pre * sig
        u = step_s[:, lanes] * x_conv
        z = z_ref[:, lanes]
        sig_z = sigmoid(z)
        silu_z = z * sig_z
        y = y_ref[:, lanes]
        scanned = y + chan[5:6] * x_conv
        gated = scanned * silu_z
        d_unit = d_unit_ref[:, lanes]
        d_gated = d_unit * chan[6:7] - coef * gated
        dz_ref[:, lanes] = (d_gated * scanned * (sig_z + silu_z * (1.0 - sig_z))).astype(bf16)
        dy = d_gated * silu_z
        stacked = jnp.concatenate([dy * first, dy * second], 0)
        d_mem = d_memory[:, lanes]
        state = state_ref[0, :, lanes]
        decays, weighted = [], []
        for h in (2 * pair, 2 * pair + 1):
            gap = jnp.minimum(running_t[h : h + 1, :] - running[:, h : h + 1], 0.0)
            decays.append(jnp.exp(gap))
            weighted.append(scores_t * decays[-1])
        d_weight = mm("d_weight", u, stacked, ((1,), (1,)))
        d_scores_t = d_scores_t + d_weight[:, :CHUNK] * decays[0] + d_weight[:, CHUNK:] * decays[1]
        tail = tail_s[:, lanes]
        du = mm("inside", jnp.concatenate(weighted, 1), stacked) + mm("du_tail", b_rows, d_mem) * tail
        d_b = d_b + mm("d_b", tail * u, d_mem, ((1,), (1,)))
        reached = reach_s[:, lanes] * dy
        d_c = d_c + mm("d_c", reached, state, ((1,), (1,)))
        end = jnp.sum(d_mem * later[:, lanes].astype(f32), 0, keepdims=True)
        later[:, lanes] = state
        d_memory[:, lanes] = kept_e[:, lanes] * d_mem + mm("d_state", c_rows, reached, ((0,), (0,)))
        gather = gather_ref[lanes, :]
        ends = ends + split_dot(jnp.broadcast_to(end, (8, PAIR)), gather)
        run_part = split_dot(seen("inside", dy) * y - seen("inside", u) * du, gather)
        step_part = split_dot(x_conv * du, gather)
        if pair == 0:
            run_grad_s[...] = run_part
            step_grad_s[...] = step_part
        else:
            run_grad_s[...] += run_part
            step_grad_s[...] += step_part
        d_conv = (chan[5:6] * dy + step_s[:, lanes] * du) * (sig + x_conv * (1.0 - sig))
        dconv_pad[0:CHUNK, lanes] = d_conv
        d_pre = chan[0:1] * d_conv
        g_chan_ref[0:1, lanes] += jnp.sum(d_conv * x_ref[:, lanes], 0, keepdims=True)
        for offset in range(1, 4):
            ahead = dconv_pad[pl.ds(offset, CHUNK), lanes] * aux[:, 2 + offset : 3 + offset]
            d_pre = d_pre + chan[offset : offset + 1] * ahead
            behind = x_pad[pl.ds(8 - offset, CHUNK), lanes] * aux[:, offset - 1 : offset]
            g_chan_ref[offset : offset + 1, lanes] += jnp.sum(d_conv * behind, 0, keepdims=True)
        dx_ref[:, lanes] = d_pre.astype(bf16)
        g_chan_ref[4:5, lanes] += jnp.sum(d_conv, 0, keepdims=True)
        g_chan_ref[5:6, lanes] += jnp.sum(dy * x_conv, 0, keepdims=True)
        g_chan_ref[6:7, lanes] += jnp.sum(d_unit * gated, 0, keepdims=True)

    d_decay = dot_exact(upper, run_grad_s[...]) + ends[0:1]
    d_step = step_grad_s[...] + head_ref[1:2, :] * d_decay
    d_raw = d_step * sigmoid(raw)
    ddt_ref[...] = d_raw.astype(bf16)
    g_head_ref[0:1, :] += jnp.sum(d_raw, 0, keepdims=True)
    g_head_ref[1:2, :] += jnp.sum(d_decay * decay, 0, keepdims=True)

    d_scores_t = jnp.where(linked, d_scores_t, 0.0)
    d_b = d_b + mm("d_scores", d_scores_t, c_rows)
    d_c = d_c + mm("d_scores", d_scores_t, b_rows, ((0,), (0,)))
    d_conv = jnp.concatenate([d_b, d_c], 1) * (sig_bc + pre_bc * sig_bc * (1.0 - sig_bc))
    dconv_bc_pad[0:CHUNK, :] = d_conv
    d_pre = taps_bc[0:1] * d_conv
    g_bc_ref[0:1, :] += jnp.sum(d_conv * bc_ref[...], 0, keepdims=True)
    for offset in range(1, 4):
        ahead = dconv_bc_pad[pl.ds(offset, CHUNK), :] * aux[:, 2 + offset : 3 + offset]
        d_pre = d_pre + taps_bc[offset : offset + 1] * ahead
        behind = bc_pad[pl.ds(8 - offset, CHUNK), :] * aux[:, offset - 1 : offset]
        g_bc_ref[offset : offset + 1, :] += jnp.sum(d_conv * behind, 0, keepdims=True)
    g_bc_ref[4:5, :] += jnp.sum(d_conv, 0, keepdims=True)
    dbc_ref[...] = d_pre.astype(bf16)
    dconv_ref[...] = dconv_pad[0:8, :]
    dconv_bc_ref[...] = dconv_bc_pad[0:8, :]


def rows_spec(width, place):
    return pl.BlockSpec((CHUNK, width), lambda i: (place(i), 0))


def within_spec(width, place):
    return pl.BlockSpec((8, width), lambda i: (jnp.maximum(place(i) * (CHUNK // 8) - 1, 0), 0))


def last_rows_spec(array):
    last = array.shape[0] // 8 - 1
    return pl.BlockSpec((8, array.shape[1]), lambda i: (last, 0))


def whole_spec(shape):
    return pl.BlockSpec(shape, lambda i: (0,) * len(shape))


def sequence_specs(segment, place, first_chunk):
    x, x_before, _, _, bc_before, dt = segment[:6]
    inner, heads = x.shape[1], dt.shape[1]
    return [
        rows_spec(inner, place),
        last_rows_spec(x_before),
        rows_spec(inner, place),
        rows_spec(2 * STATE, place),
        last_rows_spec(bc_before),
        rows_spec(heads, place),
        rows_spec(16, lambda i: place(i) + first_chunk),
        pl.BlockSpec((1, CHUNK), lambda i: (0, place(i) + first_chunk)),
        whole_spec((8, inner)),
        whole_spec((8, 2 * STATE)),
        whole_spec((8, heads)),
        whole_spec((heads, inner)),
    ]


def forward_scan(segment, start, first_chunk):
    tokens, inner = segment[0].shape
    chunks = tokens // CHUNK

    def place(i):
        return i

    return pl.pallas_call(
        forward_kernel,
        grid=(chunks,),
        in_specs=sequence_specs(segment, place, first_chunk) + [whole_spec((STATE, inner))],
        out_specs=[
            rows_spec(inner, place),
            rows_spec(inner, place),
            rows_spec(1, place),
            pl.BlockSpec((1, STATE, inner), lambda i: (i, 0, 0)),
            whole_spec((STATE, inner)),
        ],
        out_shape=[
            jax.ShapeDtypeStruct((tokens, inner), f32),
            jax.ShapeDtypeStruct((tokens, inner), bf16),
            jax.ShapeDtypeStruct((tokens, 1), f32),
            jax.ShapeDtypeStruct((chunks, STATE, inner), STATE_TYPE),
            jax.ShapeDtypeStruct((STATE, inner), f32),
        ],
        scratch_shapes=[
            pltpu.VMEM((CHUNK + 8, inner), f32),
            pltpu.VMEM((CHUNK + 8, 2 * STATE), f32),
            pltpu.VMEM((STATE, inner), f32),
            pltpu.VMEM((CHUNK, inner), f32),
            pltpu.VMEM((CHUNK, inner), f32),
            pltpu.VMEM((CHUNK, inner), f32),
        ],
        compiler_params=pltpu.CompilerParams(vmem_limit_bytes=32 << 20),
        cost_estimate=pl.CostEstimate(
            flops=tokens * inner * 2000, bytes_accessed=tokens * inner * 18, transcendentals=0
        ),
        name="forward_scan",
    )(*segment, start)


def backward_scan(segment, first_chunk, gather, y, states, next_states, d_unit, coef, carried):
    tokens, inner = segment[0].shape
    heads = segment[5].shape[1]
    chunks = tokens // CHUNK

    def place(i):
        return chunks - 1 - i

    carried_specs = [whole_spec(array.shape) for array in carried]
    return pl.pallas_call(
        backward_kernel,
        grid=(chunks,),
        in_specs=sequence_specs(segment, place, first_chunk)
        + [
            within_spec(inner, place),
            within_spec(2 * STATE, place),
            whole_spec((inner, heads)),
            rows_spec(inner, place),
            pl.BlockSpec((1, STATE, inner), lambda i: (place(i), 0, 0)),
            pl.BlockSpec((1, STATE, inner), lambda i: (0, 0, 0)),
            rows_spec(inner, place),
            rows_spec(1, place),
        ]
        + carried_specs,
        out_specs=[
            rows_spec(inner, place),
            rows_spec(inner, place),
            rows_spec(2 * STATE, place),
            rows_spec(heads, place),
        ]
        + carried_specs,
        out_shape=[
            jax.ShapeDtypeStruct((tokens, inner), bf16),
            jax.ShapeDtypeStruct((tokens, inner), bf16),
            jax.ShapeDtypeStruct((tokens, 2 * STATE), bf16),
            jax.ShapeDtypeStruct((tokens, heads), bf16),
        ]
        + [jax.ShapeDtypeStruct(array.shape, f32) for array in carried],
        scratch_shapes=[
            pltpu.VMEM((CHUNK + 8, inner), f32),
            pltpu.VMEM((CHUNK + 8, 2 * STATE), f32),
            pltpu.VMEM((CHUNK, inner), f32),
            pltpu.VMEM((CHUNK, inner), f32),
            pltpu.VMEM((CHUNK, inner), f32),
            pltpu.VMEM((CHUNK + 8, inner), f32),
            pltpu.VMEM((CHUNK + 8, 2 * STATE), f32),
            pltpu.VMEM((CHUNK, heads), f32),
            pltpu.VMEM((CHUNK, heads), f32),
            pltpu.VMEM((STATE, inner), STATE_TYPE),
        ],
        compiler_params=pltpu.CompilerParams(vmem_limit_bytes=32 << 20),
        cost_estimate=pl.CostEstimate(
            flops=tokens * inner * 4000, bytes_accessed=tokens * inner * 26, transcendentals=0
        ),
        name="backward_scan",
    )(*segment, segment[0], segment[3], gather, y, states, next_states, d_unit, coef, *carried)


def backward_start(inner, heads):
    return [
        jnp.zeros(shape, f32)
        for shape in [(STATE, inner), (8, inner), (8, 2 * STATE), (8, inner), (8, 2 * STATE), (8, heads)]
    ]


def token_masks(segment_ids):
    length = segment_ids.shape[0]
    token = jnp.arange(length, dtype=jnp.int32)
    position = token % SEQ_LEN
    ids = segment_ids
    padded = jnp.concatenate([jnp.full((3,), -1, jnp.int32), ids, jnp.full((3,), -1, jnp.int32)])
    columns = []
    for offset in range(1, 4):
        columns.append((position >= offset) & (padded[3 - offset : 3 - offset + length] == ids))
    for offset in range(1, 4):
        columns.append(
            (position < SEQ_LEN - offset) & (padded[3 + offset : 3 + offset + length] == ids)
        )
    by_chunk = ids.reshape(-1, CHUNK)
    final = by_chunk[:, -1:]
    previous = jnp.concatenate([jnp.full((1, 1), -1, jnp.int32), final[:-1]], 0)
    start = jnp.arange(by_chunk.shape[0], dtype=jnp.int32)[:, None] * CHUNK
    previous = jnp.where(start % SEQ_LEN == 0, -1, previous)
    columns.append((by_chunk == previous).reshape(-1))
    columns.append((by_chunk == final).reshape(-1))
    columns.append(jnp.broadcast_to(final == previous, by_chunk.shape).reshape(-1))
    columns.append(ids)
    columns = columns + [jnp.zeros((length,), f32)] * (16 - len(columns))
    return jnp.stack([column.astype(f32) for column in columns], 1)


def contract_rows(left, right):
    return dot(left, right, ((0,), (0,)))


def contract_cols(left, right):
    return dot(left, right, ((1,), (1,)))


INWARD = [(0, 1), (3, 2)]
ACROSS = [(1, 2), (2, 1)]
OUTWARD = [(1, 0), (2, 3)]


class LineSum:
    def __init__(self, chains):
        me = lax.axis_index("tensor")
        self.outer = (me == 0) | (me == 3)
        self.waiting = []
        self.chains = [[None, None, None] for _ in range(chains)]
        self.sent = [[None, None, None] for _ in range(chains)]
        self.names = [[None, None, None] for _ in range(chains)]
        self.next = 0
        self.results = {}

    def add(self, name, piece):
        self.waiting.append((name, piece))

    def busy(self):
        return bool(self.waiting) or any(part is not None for chain in self.chains for part in chain)

    def turn(self, carried=()):
        chain = self.next
        self.next = (chain + 1) % len(self.chains)
        held, sent, names = self.chains[chain], self.sent[chain], self.names[chain]
        name, piece = self.waiting.pop(0) if self.waiting else (None, None)
        tied = lax.optimization_barrier((tuple(sent), piece, tuple(carried)))
        sent, piece, carried = tied
        inward = None if held[0] is None else held[0] + sent[0]
        across = None if held[1] is None else held[1] + sent[1]
        if held[2] is not None:
            self.results[names[2]] = jnp.where(self.outer, sent[2], held[2])
        self.chains[chain] = [piece, inward, across]
        self.names[chain] = [name, names[0], names[1]]
        self.sent[chain] = [
            None if part is None else lax.ppermute(part, "tensor", route)
            for part, route in zip(self.chains[chain], (INWARD, ACROSS, OUTWARD))
        ]
        return carried


SEGMENT = 256
PIECE = 128
CHAINS = 2


def shards(
    tensor_size,
    hidden_in,
    norm_gain,
    z_weight,
    x_weight,
    bc_weight,
    dt_weight,
    conv_x,
    conv_x_bias,
    conv_bc,
    conv_bc_bias,
    dt_bias,
    a_log,
    d_skip,
    gate_gain,
    out_weight,
    cotangent,
    segment_ids,
):
    tokens, width = hidden_in.shape
    heads = dt_bias.shape[0]
    inner = heads * HEAD
    count = tokens // SEGMENT
    chunks = SEGMENT // CHUNK
    line = LineSum(CHAINS)

    rate = -jnp.exp(a_log)
    zero_row = jnp.zeros((1, inner), f32)
    chan = jnp.concatenate(
        [conv_x, conv_x_bias[None], jnp.repeat(d_skip, HEAD)[None], gate_gain[None], zero_row], 0
    )
    taps_bc = jnp.concatenate([conv_bc, conv_bc_bias[None], jnp.zeros((3, 2 * STATE), f32)], 0)
    head_rows = jnp.concatenate([dt_bias[None], rate[None], jnp.zeros((6, heads), f32)], 0)
    owner = jnp.arange(inner, dtype=jnp.int32) // HEAD
    spread = (jnp.arange(heads, dtype=jnp.int32)[:, None] == owner[None, :]).astype(bf16)
    gather = (owner[:, None] == jnp.arange(heads, dtype=jnp.int32)[None, :]).astype(bf16)
    shared = (
        token_masks(segment_ids), segment_ids.astype(f32)[None], chan, taps_bc, head_rows, spread,
    )

    def rows(array, index):
        return lax.slice_in_dim(array, index * SEGMENT, (index + 1) * SEGMENT, axis=0)

    def split(array):
        return [array[at : at + PIECE] for at in range(0, SEGMENT, PIECE)]

    memory = jnp.zeros((STATE, inner), f32)
    segments, normed, hats, rms, ys, units, states, stats = [], [], [], [], [], [], [], []
    for index in range(count):
        hidden = rows(hidden_in, index)
        if index:
            memory, hidden = line.turn((memory, hidden))
        base = hidden.astype(f32)
        rms.append(lax.rsqrt(jnp.mean(base * base, -1, keepdims=True) + epsilon))
        normed.append((base * rms[-1] * norm_gain[None, :]).astype(bf16))
        x_pre = dot(normed[-1], x_weight)
        bc_pre = dot(normed[-1], bc_weight)
        z_pre = dot(normed[-1], z_weight)
        dt_pre = dot(normed[-1], dt_weight)
        before = segments[-1] if segments else (x_pre, None, None, bc_pre)
        segments.append((x_pre, before[0], z_pre, bc_pre, before[3], dt_pre) + shared)
        y, unit, squares, state, memory = forward_scan(segments[-1], memory, index * chunks)
        proj = dot(unit, out_weight)
        for number, piece in enumerate(split(proj)):
            line.add(("out", index * SEGMENT + number * PIECE), piece)
        share = jnp.sum(rows(cotangent, index).astype(f32) * proj, -1)
        stats.append(jnp.concatenate([squares.T, share[None]], 0))
        ys.append(y)
        units.append(unit)
        states.append(state)

    (local,) = line.turn((jnp.concatenate(stats, 1),))
    total = lax.psum(local, "tensor")
    (total,) = line.turn((total,))
    scale = lax.rsqrt(total[0] / D_INNER + epsilon)[:, None]
    d_scale = total[1][:, None]
    coef = d_scale * scale * scale * scale / D_INNER
    d_proj = (scale * cotangent.astype(f32)).astype(bf16)

    carried = backward_start(inner, heads)
    grads = [None] * count
    norm_grad = jnp.zeros((width,), f32)
    for index in reversed(range(count)):
        d_unit = contract_cols(rows(d_proj, index), out_weight)
        outs = backward_scan(
            segments[index], index * chunks, gather, ys[index], states[index],
            states[min(index + 1, count - 1)], d_unit, rows(coef, index), carried,
        )
        d_z, d_x, d_bc, d_dt = grads[index] = outs[:4]
        carried = outs[4:]
        part = (
            contract_cols(d_z, z_weight)
            + contract_cols(d_x, x_weight)
            + contract_cols(d_dt, dt_weight)
            + contract_cols(d_bc, bc_weight)
        )
        base = rows(hidden_in, index).astype(f32)
        norm_grad = norm_grad + jnp.sum(part * (base * rms[index]), 0)
        for number, piece in reversed(list(enumerate(split(part)))):
            line.add(("in", index * SEGMENT + number * PIECE), piece)
        *carried, norm_grad = line.turn(tuple(carried) + (norm_grad,))

    normed_all = jnp.concatenate(normed, 0)
    unit_all = jnp.concatenate(units, 0)
    d_z, d_x, d_bc, d_dt = [jnp.concatenate([g[k] for g in grads], 0) for k in range(4)]
    d_rest = jnp.concatenate([d_bc, d_dt], 1)
    rest_share = lax.psum_scatter(
        contract_rows(normed_all, d_rest), "dp", scatter_dimension=0, tiled=True
    )
    out_share = lax.psum_scatter(
        contract_rows(unit_all, d_proj), "dp", scatter_dimension=1, tiled=True
    )
    z_share = lax.psum_scatter(contract_rows(normed_all, d_z), "dp", scatter_dimension=0, tiled=True)
    x_share = lax.psum_scatter(contract_rows(normed_all, d_x), "dp", scatter_dimension=0, tiled=True)
    norm_grad, g_chan, g_bc, g_head = lax.psum((norm_grad,) + tuple(carried[3:]), "dp")

    bc_part = rest_share[:, : 2 * STATE]
    extra = jnp.concatenate([norm_grad, g_bc.reshape(-1), bc_part.reshape(-1)])
    extra_rows = -(-extra.shape[0] // (8 * width)) * 8
    extra = jnp.pad(extra, (0, extra_rows * width - extra.shape[0])).reshape(extra_rows, width)
    line.add(("extra", 0), extra)

    output = jnp.zeros((tokens, width), f32)
    input_grad = jnp.zeros((tokens, width), f32)
    done = 0
    while line.busy():
        line.turn()
    for (kind, at), value in line.results.items():
        if kind == "extra":
            flat = value.reshape(-1)
            norm_gain_grad = flat[:width]
            g_bc = flat[width : width + g_bc.size].reshape(g_bc.shape)
            begin = width + g_bc.size
            bc_share = flat[begin : begin + bc_part.size].reshape(bc_part.shape)
            continue
        base = hidden_in[at : at + PIECE].astype(f32)
        if kind == "out":
            result = base + scale[at : at + PIECE] * value
            output = lax.dynamic_update_slice(output, result, (at, 0))
        else:
            cot = cotangent[at : at + PIECE].astype(f32)
            inverse = rms[at // SEGMENT][at % SEGMENT : at % SEGMENT + PIECE]
            hat = base * inverse
            d_hat = value * norm_gain[None, :]
            result = cot + inverse * (d_hat - hat * jnp.mean(d_hat * hat, -1, keepdims=True))
            input_grad = lax.dynamic_update_slice(input_grad, result, (at, 0))
    return (
        output,
        input_grad,
        norm_gain_grad,
        z_share,
        x_share,
        bc_share,
        rest_share[:, 2 * STATE :],
        g_chan[:4],
        g_chan[4],
        g_bc[:4],
        g_bc[4],
        g_head[0],
        g_head[1],
        jnp.sum(g_chan[5].reshape(heads, HEAD), 1),
        g_chan[6],
        out_share,
    )


def solution(mesh):
    placed = (
        P("dp", None),
        P(),
        P(None, "tensor"),
        P(None, "tensor"),
        P(),
        P(None, "tensor"),
        P(None, "tensor"),
        P("tensor"),
        P(),
        P(),
        P("tensor"),
        P("tensor"),
        P("tensor"),
        P("tensor"),
        P("tensor", None),
        P("dp", None),
        P("dp"),
    )
    return jax.shard_map(
        partial(shards, mesh.shape["tensor"]),
        mesh=mesh,
        in_specs=placed,
        out_specs=(
            P("dp", None),
            P("dp", None),
            P(),
            P("dp", "tensor"),
            P("dp", "tensor"),
            P("dp", None),
            P("dp", "tensor"),
            P(None, "tensor"),
            P("tensor"),
            P(),
            P(),
            P("tensor"),
            P("tensor"),
            P("tensor"),
            P("tensor"),
            P("tensor", "dp"),
        ),
        check_vma=False,
    )
```

time: 1440 us -> 702 us (0.49)
  waiting for transfers between devices: 821 us -> 60.6 us
  starting transfers between devices: 0.29 us -> 194 us
  matrix products: 261 us -> 112 us
  local copies, waits for them, and re-layouts: 159 us -> 84.4 us
  Pallas kernels: 0 us -> 66 us
  loops' own time: 27.7 us -> 0 us
    psum x2 -> x0, waiting for transfers between devices: 587 us -> none  [the longest x1 309 us: shards(): lax.psum((normed_part, d_bc_conv_part), 'tensor')]
    reduce_scatter x5 -> x4, waiting for transfers between devices: 234 us -> 0.01 us  [the longest x1 0.01 us: shards(): lax.psum_scatter(contract_rows(normed_all, d_rest), 'dp', scatter_dimensi...]
    ppermute x0 -> x51, starting transfers between devices: none -> 193 us  [turn(): lax.ppermute(part, 'tensor', route)]
    dot_general x63 -> x44, matrix products: 250 us -> 112 us  [dot(): lax.dot_general(left, right, (dims, ((), ())), preferred_element_type=f32)]
    pallas_call x0 -> x8, Pallas kernels: none -> 66 us  [the longest x4 46 us: backward_scan(): pl.pallas_call(backward_kernel, grid=(chunks,), in_specs=sequence_specs(s...]
    ppermute x0 -> x51, waiting for transfers between devices: none -> 60.6 us  [turn(): lax.ppermute(part, 'tensor', route)]
    add x1 -> x38, other arithmetic: 10.5 us -> 63.4 us  [the longest x17 33.3 us: turn(): inward = None if held[0] is None else held[0] + sent[0]]
    reshape x11 -> x2, local copies, waits for them, and re-layouts: 47.3 us -> 1.53 us  [the longest x1 0.78 us: shards(): jnp.pad(extra, (0, extra_rows * width - extra.shape[0]))]
  transfers between devices with their start and end apart: 7 -> 55, of which waited for: 6 -> 10; matrix products, arithmetic and copies ran while one was open for 4% -> 34% of each run, Pallas kernels for 0% -> 7%
where the time goes in v1:
time: 702 us; the launch traced here: 693 us
  starting transfers between devices  194 us (28%)
  matrix products  112 us (16%)
  other arithmetic  107 us (15%)
  local copies, waits for them, and re-layouts  84.4 us (12%)
  Pallas kernels  66 us (9%)
  waiting for transfers between devices  60.6 us (9%)
  blocking collectives  50.7 us (7%)
  between operations  17.8 us (3%)
    ppermute x51, starting transfers between devices, turn(): lax.ppermute(part, 'tensor', route)  193 us
    dot_general x44, matrix products, dot(): lax.dot_general(left, right, (dims, ((), ())), preferred_element_type=f32)  112 us
    ppermute x51, waiting for transfers between devices, turn(): lax.ppermute(part, 'tensor', route)  60.6 us
    pallas_call x4, Pallas kernels, backward_scan(): pl.pallas_call(backward_kernel, grid=(chunks,), in_specs=sequence_specs(s...  46 us
    unnamed x516, local copies, waits for them, and re-layouts  43.8 us
    add x17, other arithmetic, turn(): inward = None if held[0] is None else held[0] + sent[0]  33.3 us
    psum x1, blocking collectives, shards(): total = lax.psum(local, 'tensor')  27.9 us
    add x17, other arithmetic, turn(): across = None if held[1] is None else held[1] + sent[1]  26.2 us
  transfers between devices with their start and end apart: 55, of which 10 were waited for; matrix products, arithmetic and copies ran while one was open for 34% of the time, Pallas kernels for 7%

profile of v1, /device:TPU:0, one launch (start us, length us, event | category | flops | bytes accessed | tf_op | source)
XLA Modules:
  0.0 692.9 jit_solution(2578758269168684340)
XLA Ops:
  32.5 6.7 collective-permute-start
  44.2 4.8 forward_scan.5
  62.2 5.1 fusion.193
  67.3 4.8 forward_scan.6
  97.7 5.6 forward_scan.7
  107.8 8.2 %multiply_reduce_fusion.6 = (f32[256]{0:T(256)S(1)}, f32[256]{0:T(256)S(1)}, f32[256]{0:T(256)S(1)}, f32[256]{0:T(256)S(1)}, f32[256,2048]{1,0:T(8,128)}) fusion(f32[256,2048]{1,0:T(8,128)} %copy-done.164, bf16[1024,2048]{1,0:T(8,128)(2,1)} %param.32, f32[256,2048]{1,0:T(8,128)} %copy-done.166, f32[256,2048]{1,0:T(8,128)} %fusion.193, ...), kind=kOutput, calls=%fused_computation.66 | convolution fusion | flops 1080032256 | bytes 17305600 | tf_op jit(solution)/shard_map/dot_general | solution.py:24
  122.6 27.9 %psum.35 = f32[2,1024]{1,0:T(2,128)S(1)} all-reduce(f32[2,1024]{1,0:T(2,128)S(1)} %maximum_maximum_fusion.1), channel_id=1, replica_groups=mesh['dp'=8,'tensor'=4] {'tensor'}, use_global_device_ids=true, to_apply=%region_8.9 | all-reduce | flops 2048 | bytes 16384 | tf_op jit(solution)/shard_map/psum | solution.py:614
  166.1 6.5 collective-permute-start.4
  180.4 11.6 %backward_scan.4 = (bf16[256,1024]{1,0:T(8,128)(2,1)S(1)}, bf16[256,1024]{1,0:T(8,128)(2,1)S(1)}, bf16[256,256]{1,0:T(8,128)(2,1)S(1)}, bf16[256,16]{1,0:T(8,128...) custom-call(f32[256,1024]{1,0:T(8,128)S(1)} %copy-done.13, ...), custom_call_target="tpu_custom_call" | custom-call | flops 1048576000 | bytes 6815744 | tf_op jit(solution)/shard_map/backward_scan/pallas_call | solution.py:404
  216.7 11.2 %backward_scan.5 = (bf16[256,1024]{1,0:T(8,128)(2,1)S(1)}, bf16[256,1024]{1,0:T(8,128)(2,1)S(1)}, bf16[256,256]{1,0:T(8,128)(2,1)S(1)}, bf16[256,16]{1,0:T(8,128...) custom-call(f32[256,1024]{1,0:T(8,128)S(1)} %copy-done.8, ...), custom_call_target="tpu_custom_call" | custom-call | flops 1048576000 | bytes 6815744 | tf_op jit(solution)/shard_map/backward_scan/pallas_call | solution.py:404
  250.8 6.6 collective-permute-start.9
  257.6 11.2 %backward_scan.6 = (bf16[256,1024]{1,0:T(8,128)(2,1)S(1)}, bf16[256,1024]{1,0:T(8,128)(2,1)S(1)}, bf16[256,256]{1,0:T(8,128)(2,1)S(1)}, bf16[256,16]{1,0:T(8,128...) custom-call(f32[256,1024]{1,0:T(8,128)S(1)} %copy-done.4, ...), custom_call_target="tpu_custom_call" | custom-call | flops 1048576000 | bytes 6815744 | tf_op jit(solution)/shard_map/backward_scan/pallas_call | solution.py:404
  282.7 12.0 %backward_scan.7 = (bf16[256,1024]{1,0:T(8,128)(2,1)S(1)}, bf16[256,1024]{1,0:T(8,128)(2,1)S(1)}, bf16[256,256]{1,0:T(8,128)(2,1)S(1)}, bf16[256,16]{1,0:T(8,128...) custom-call(f32[256,1024]{1,0:T(8,128)S(1)} %fusion.184.x_ref.x_befo, ...), custom_call_target="tpu_custom_call" | custom-call | flops 1048576000 | bytes 6815744 | tf_op jit(solution)/shard_map/backward_scan/pallas_call | solution.py:404
  299.1 5.2 fusion.112
  304.4 9.0 %fusion.34 = f32[1024,2048]{1,0:T(8,128)} fusion(bf16[1024,2048]{1,0:T(8,128)(2,1)} %copy-done.190, bf16[256,1024]{1,0:T(8,128)(2,1)S(1)} %copy-done.78, bf16[256,1024]{1,0:T(8,128)(2,1)S(1)} %copy-done.135, bf16[256,1024]{1,0:T(8,128)(2,1)S(1)} %copy-done.131, bf16[256,1024]{1,0:T(8,128)(2,1)S(1)} %copy-done.129), kind=kOutput, calls=%fused_computation.52 | convolution fusion | flops 4303355904 | bytes 14680064 | tf_op jit(solution)/shard_map/dot_general | solution.py:24
  315.0 10.0 %fusion.26 = f32[2048,1024]{1,0:T(8,128)} fusion(bf16[256,1024]{1,0:T(8,128)(2,1)S(1)} %copy-done.59, bf16[256,1024]{1,0:T(8,128)(2,1)S(1)} %copy-done.62, bf16[256,1024]{1,0:T(8,128)(2,1)S(1)} %copy-done.66, bf16[256,1024]{1,0:T(8,128)(2,1)S(1)} %copy-done.64, bf16[256,2048]{1,0:T(8,128)(2,1)} %copy-done.154, bf16[256,2048]{1,0:T(8,128)(2,1)} %copy-done.152, ...), kind=kOutput, calls=%fused_computation.44 | convolution fusion | flops 4320133120 | bytes 14680064 | tf_op jit(solution)/shard_map/dot_general | solution.py:24
  349.9 9.3 %collective-permute-start.15 = (f32[128,2048]{1,0:T(8,128)S(1)}, f32[128,2048]{1,0:T(8,128)S(1)}, u32[]{:S(2)}, u32[]{:S(2)}) collective-permute-start(f32[128,2048]{1,0:T(8,128)S(1)} %copy-done.187), channel_id=1, source_target_pairs={{0,1},{3,2},{4,5},{7,6},{8,9},{11,10},{12,13},{15,14},{16,17},{19,... | collective-permute-start | bytes 3145736 | tf_op jit(solution)/shard_map/ppermute | solution.py:530
  363.4 18.4 %collective-permute-start.18 = (f32[128,2048]{1,0:T(8,128)S(1)}, f32[128,2048]{1,0:T(8,128)S(1)}, u32[]{:S(2)}, u32[]{:S(2)}) collective-permute-start(f32[128,2048]{1,0:T(8,128)S(1)} %get-tuple-element.278), channel_id=1, source_target_pairs={{0,1},{3,2},{4,5},{7,6},{8,9},{11,10},{12,13},{15,14},{16,17},{19,... | collective-permute-start | bytes 3145736 | tf_op jit(solution)/shard_map/ppermute | solution.py:530
  385.6 18.6 %collective-permute-start.21 = (f32[128,2048]{1,0:T(8,128)S(1)}, f32[128,2048]{1,0:T(8,128)S(1)}, u32[]{:S(2)}, u32[]{:S(2)}) collective-permute-start(f32[128,2048]{1,0:T(8,128)S(1)} %get-tuple-element.282), channel_id=1, source_target_pairs={{0,1},{3,2},{4,5},{7,6},{8,9},{11,10},{12,13},{15,14},{16,17},{19,... | collective-permute-start | bytes 3145736 | tf_op jit(solution)/shard_map/ppermute | solution.py:530
  411.3 16.2 %collective-permute-start.24 = (f32[128,2048]{1,0:T(8,128)}, f32[128,2048]{1,0:T(8,128)}, u32[]{:S(2)}, u32[]{:S(2)}) collective-permute-start(f32[128,2048]{1,0:T(8,128)} %get-tuple-element.286), channel_id=1, source_target_pairs={{0,1},{3,2},{4,5},{7,6},{8,9},{11,10},{12,13},{15,14},{16,17},{19,... | collective-permute-start | bytes 3145736 | tf_op jit(solution)/shard_map/ppermute | solution.py:530
  431.0 9.0 %fusion.18 = f32[2048,1024]{1,0:T(8,128)} fusion(bf16[256,1024]{1,0:T(8,128)(2,1)S(1)} %copy-done.127, bf16[256,1024]{1,0:T(8,128)(2,1)S(1)} %copy-done.133, bf16[256,1024]{1,0:T(8,128)(2,1)S(1)} %copy-done.137, bf16[256,1024]{1,0:T(8,128)(2,1)S(1)} %copy-done.139, bf16[256,2048]{1,0:T(8,128)(2,1)S(1)} %copy-done.155, ...), kind=kOutput, calls=%fused_computation.36 | convolution fusion | flops 4320133120 | bytes 14680064 | tf_op jit(solution)/shard_map/dot_general | solution.py:24
  445.6 6.6 collective-permute-start.27
  458.5 14.2 %collective-permute-start.30 = (f32[128,2048]{1,0:T(8,128)}, f32[128,2048]{1,0:T(8,128)}, u32[]{:S(2)}, u32[]{:S(2)}) collective-permute-start(f32[128,2048]{1,0:T(8,128)} %get-tuple-element.294), channel_id=1, source_target_pairs={{0,1},{3,2},{4,5},{7,6},{8,9},{11,10},{12,13},{15,14},{16,17},{19,... | collective-permute-start | bytes 3145736 | tf_op jit(solution)/shard_map/ppermute | solution.py:530
  484.2 10.9 %collective-permute-start.33 = (f32[128,2048]{1,0:T(8,128)}, f32[128,2048]{1,0:T(8,128)}, u32[]{:S(2)}, u32[]{:S(2)}) collective-permute-start(f32[128,2048]{1,0:T(8,128)} %get-tuple-element.298), channel_id=1, source_target_pairs={{0,1},{3,2},{4,5},{7,6},{8,9},{11,10},{12,13},{15,14},{16,17},{19,... | collective-permute-start | bytes 3145736 | tf_op jit(solution)/shard_map/ppermute | solution.py:530
  501.7 22.8 %all-reduce.5 = (f32[2048]{0:T(1024)S(1)}, f32[2048]{0:T(1024)S(1)}, f32[8,1024]{1,0:T(8,128)S(1)}, f32[8,16]{1,0:T(8,128)S(1)}) all-reduce(f32[2048]{0:T(1024)S(1)} %bitcast.161, f32[2048]{0:T(1024)S(1)} %add.368, f32[8,1024]{1,0:T(8,128)S(1)} %copy-done.103, f32[8,16]{1,0:T(8,128)S(1)} %copy-done.125), channel_id=1, replica_groups=mesh['dp'=8,'tensor'=4] {'dp'}, use_global_device_ids=true, to_apply=%region_16.17 | all-reduce | flops 12416 | bytes 99328 | tf_op jit(solution)/shard_map/psum | solution.py:656
  534.1 6.8 collective-permute-start.36
  549.1 8.8 %collective-permute-start.39 = (f32[128,2048]{1,0:T(8,128)}, f32[128,2048]{1,0:T(8,128)}, u32[]{:S(2)}, u32[]{:S(2)}) collective-permute-start(f32[128,2048]{1,0:T(8,128)} %get-tuple-element.308), channel_id=1, source_target_pairs={{0,1},{3,2},{4,5},{7,6},{8,9},{11,10},{12,13},{15,14},{16,17},{19,... | collective-permute-start | bytes 3145736 | tf_op jit(solution)/shard_map/ppermute | solution.py:530
  568.3 5.4 collective-permute-start.42
  576.7 9.6 %collective-permute-done.39 = f32[128,2048]{1,0:T(8,128)} collective-permute-done((f32[128,2048]{1,0:T(8,128)}, f32[128,2048]{1,0:T(8,128)}, u32[]{:S(2)}, u32[]{:S(2)}) %collective-permute-start.39) | collective-permute-done | bytes 1048608 | tf_op jit(solution)/shard_map/ppermute | solution.py:530
  610.9 10.9 %collective-permute-done.46 = f32[128,2048]{1,0:T(8,128)} collective-permute-done((f32[128,2048]{1,0:T(8,128)S(1)}, f32[128,2048]{1,0:T(8,128)}, u32[]{:S(2)}, u32[]{:S(2)}) %collective-permute-start.46) | collective-permute-done | bytes 1048608 | tf_op jit(solution)/shard_map/ppermute | solution.py:530
  633.6 10.6 %collective-permute-done.48 = f32[128,2048]{1,0:T(8,128)S(1)} collective-permute-done((f32[128,2048]{1,0:T(8,128)S(1)}, f32[128,2048]{1,0:T(8,128)S(1)}, u32[]{:S(2)}, u32[]{:S(2)}) %collective-permute-start.48) | collective-permute-done | bytes 1048608 | tf_op jit(solution)/shard_map/ppermute | solution.py:530
  645.5 19.6 %collective-permute-done.49 = f32[128,2048]{1,0:T(8,128)S(1)} collective-permute-done((f32[128,2048]{1,0:T(8,128)S(1)}, f32[128,2048]{1,0:T(8,128)S(1)}, u32[]{:S(2)}, u32[]{:S(2)}) %collective-permute-start.49) | collective-permute-done | bytes 1048608 | tf_op jit(solution)/shard_map/ppermute | solution.py:530
  (796 shorter events, 331.0 us)
Async XLA Ops:
  7.2 519.6 %reduce-scatter.5.cloned.1.call-start = ((), (), s32[]{:S(2)}) async-start(), calls=%async_computation.4 | async-start | bytes 2506752 | tf_op jit(solution)/shard_map/reduce_scatter | solution.py:648
  32.5 52.2 %collective-permute-start = (f32[128,2048]{1,0:T(8,128)}, f32[128,2048]{1,0:T(8,128)}, u32[]{:S(2)}, u32[]{:S(2)}) collective-permute-start(f32[128,2048]{1,0:T(8,128)} %get-tuple-element.173), channel_id=1, source_target_pairs={{0,1},{3,2},{4,5},{7,6},{8,9},{11,10},{12,13},{15,14},{16,17},{19,... | collective-permute-start | bytes 3145736 | tf_op jit(solution)/shard_map/ppermute | solution.py:530
  49.0 67.0 %collective-permute-start.3 = (f32[128,2048]{1,0:T(8,128)}, f32[128,2048]{1,0:T(8,128)}, u32[]{:S(2)}, u32[]{:S(2)}) collective-permute-start(f32[128,2048]{1,0:T(8,128)} %get-tuple-element.184), channel_id=1, source_target_pairs={{0,1},{3,2},{4,5},{7,6},{8,9},{11,10},{12,13},{15,14},{16,17},{19,... | collective-permute-start | bytes 3145736 | tf_op jit(solution)/shard_map/ppermute | solution.py:530
  93.1 60.6 %collective-permute-start.2 = (f32[128,2048]{1,0:T(8,128)}, f32[128,2048]{1,0:T(8,128)}, u32[]{:S(2)}, u32[]{:S(2)}) collective-permute-start(f32[128,2048]{1,0:T(8,128)} %add.341), channel_id=1, source_target_pairs={{1,2},{2,1},{5,6},{6,5},{9,10},{10,9},{13,14},{14,13},{17,18},{18,... | collective-permute-start | bytes 3145736 | tf_op jit(solution)/shard_map/ppermute | solution.py:530
  94.8 58.9 %collective-permute-start.1 = (f32[128,2048]{1,0:T(8,128)}, f32[128,2048]{1,0:T(8,128)}, u32[]{:S(2)}, u32[]{:S(2)}) collective-permute-start(f32[128,2048]{1,0:T(8,128)} %get-tuple-element.181), channel_id=1, source_target_pairs={{0,1},{3,2},{4,5},{7,6},{8,9},{11,10},{12,13},{15,14},{16,17},{19,... | collective-permute-start | bytes 3145736 | tf_op jit(solution)/shard_map/ppermute | solution.py:530
  118.7 92.3 %collective-permute-start.8 = (f32[128,2048]{1,0:T(8,128)}, f32[128,2048]{1,0:T(8,128)}, u32[]{:S(2)}, u32[]{:S(2)}) collective-permute-start(f32[128,2048]{1,0:T(8,128)} %add.347), channel_id=1, source_target_pairs={{1,2},{2,1},{5,6},{6,5},{9,10},{10,9},{13,14},{14,13},{17,18},{18,... | collective-permute-start | bytes 3145736 | tf_op jit(solution)/shard_map/ppermute | solution.py:530
  120.4 90.7 %collective-permute-start.7 = (f32[128,2048]{1,0:T(8,128)}, f32[128,2048]{1,0:T(8,128)}, u32[]{:S(2)}, u32[]{:S(2)}) collective-permute-start(f32[128,2048]{1,0:T(8,128)} %get-tuple-element.200), channel_id=1, source_target_pairs={{0,1},{3,2},{4,5},{7,6},{8,9},{11,10},{12,13},{15,14},{16,17},{19,... | collective-permute-start | bytes 3145736 | tf_op jit(solution)/shard_map/ppermute | solution.py:530
  163.2 87.6 %collective-permute-start.5 = (f32[128,2048]{1,0:T(8,128)}, f32[128,2048]{1,0:T(8,128)}, u32[]{:S(2)}, u32[]{:S(2)}) collective-permute-start(f32[128,2048]{1,0:T(8,128)} %add.345), channel_id=1, source_target_pairs={{1,2},{2,1},{5,6},{6,5},{9,10},{10,9},{13,14},{14,13},{17,18},{18,... | collective-permute-start | bytes 3145736 | tf_op jit(solution)/shard_map/ppermute | solution.py:530
  164.8 92.6 %collective-permute-start.6 = (f32[128,2048]{1,0:T(8,128)}, f32[128,2048]{1,0:T(8,128)}, u32[]{:S(2)}, u32[]{:S(2)}) collective-permute-start(f32[128,2048]{1,0:T(8,128)} %add.346), channel_id=1, source_target_pairs={{1,0},{2,3},{5,4},{6,7},{9,8},{10,11},{13,12},{14,15},{17,16},{18,... | collective-permute-start | bytes 3145736 | tf_op jit(solution)/shard_map/ppermute | solution.py:530
  166.1 91.3 %collective-permute-start.4 = (f32[128,2048]{1,0:T(8,128)}, f32[128,2048]{1,0:T(8,128)}, u32[]{:S(2)}, u32[]{:S(2)}) collective-permute-start(f32[128,2048]{1,0:T(8,128)} %get-tuple-element.194), channel_id=1, source_target_pairs={{0,1},{3,2},{4,5},{7,6},{8,9},{11,10},{12,13},{15,14},{16,17},{19,... | collective-permute-start | bytes 3145736 | tf_op jit(solution)/shard_map/ppermute | solution.py:530
  234.6 47.9 %collective-permute-start.10 = (f32[128,2048]{1,0:T(8,128)}, f32[128,2048]{1,0:T(8,128)}, u32[]{:S(2)}, u32[]{:S(2)}) collective-permute-start(f32[128,2048]{1,0:T(8,128)} %add.356), channel_id=1, source_target_pairs={{1,2},{2,1},{5,6},{6,5},{9,10},{10,9},{13,14},{14,13},{17,18},{18,... | collective-permute-start | bytes 3145736 | tf_op jit(solution)/shard_map/ppermute | solution.py:530
  236.3 46.3 %collective-permute-start.11 = (f32[128,2048]{1,0:T(8,128)}, f32[128,2048]{1,0:T(8,128)}, u32[]{:S(2)}, u32[]{:S(2)}) collective-permute-start(f32[128,2048]{1,0:T(8,128)} %add.357), channel_id=1, source_target_pairs={{1,0},{2,3},{5,4},{6,7},{9,8},{10,11},{13,12},{14,15},{17,16},{18,... | collective-permute-start | bytes 3145736 | tf_op jit(solution)/shard_map/ppermute | solution.py:530
  304.3 381.6 %reduce-scatter.11.cloned.1.call-start = ((), (), s32[]{:S(2)}) async-start(), calls=%async_computation.7 | async-start | bytes 9437184 | tf_op jit(solution)/shard_map/reduce_scatter | solution.py:651
  313.4 372.5 %reduce-scatter.9.cloned.1.call-start = ((), (), s32[]{:S(2)}) async-start(), calls=%async_computation.6 | async-start | bytes 9437184 | tf_op jit(solution)/shard_map/reduce_scatter | solution.py:655
  325.0 360.8 %reduce-scatter.7.cloned.1.call-start = ((), (), s32[]{:S(2)}) async-start(), calls=%async_computation.5 | async-start | bytes 9437184 | tf_op jit(solution)/shard_map/reduce_scatter | solution.py:654
  341.4 40.3 %collective-permute-start.17 = (f32[128,2048]{1,0:T(8,128)S(1)}, f32[128,2048]{1,0:T(8,128)S(1)}, u32[]{:S(2)}, u32[]{:S(2)}) collective-permute-start(f32[128,2048]{1,0:T(8,128)S(1)} %add.371), channel_id=1, source_target_pairs={{1,0},{2,3},{5,4},{6,7},{9,8},{10,11},{13,12},{14,15},{17,16},{18,... | collective-permute-start | bytes 3145736 | tf_op jit(solution)/shard_map/ppermute | solution.py:530
  361.9 43.8 %collective-permute-start.20 = (f32[128,2048]{1,0:T(8,128)S(1)}, f32[128,2048]{1,0:T(8,128)S(1)}, u32[]{:S(2)}, u32[]{:S(2)}) collective-permute-start(f32[128,2048]{1,0:T(8,128)S(1)} %add.374), channel_id=1, source_target_pairs={{1,0},{2,3},{5,4},{6,7},{9,8},{10,11},{13,12},{14,15},{17,16},{18,... | collective-permute-start | bytes 3145736 | tf_op jit(solution)/shard_map/ppermute | solution.py:530
  363.4 42.4 %collective-permute-start.18 = (f32[128,2048]{1,0:T(8,128)S(1)}, f32[128,2048]{1,0:T(8,128)S(1)}, u32[]{:S(2)}, u32[]{:S(2)}) collective-permute-start(f32[128,2048]{1,0:T(8,128)S(1)} %get-tuple-element.278), channel_id=1, source_target_pairs={{0,1},{3,2},{4,5},{7,6},{8,9},{11,10},{12,13},{15,14},{16,17},{19,... | collective-permute-start | bytes 3145736 | tf_op jit(solution)/shard_map/ppermute | solution.py:530
  384.3 43.3 %collective-permute-start.23 = (f32[128,2048]{1,0:T(8,128)S(1)}, f32[128,2048]{1,0:T(8,128)S(1)}, u32[]{:S(2)}, u32[]{:S(2)}) collective-permute-start(f32[128,2048]{1,0:T(8,128)S(1)} %add.377), channel_id=1, source_target_pairs={{1,0},{2,3},{5,4},{6,7},{9,8},{10,11},{13,12},{14,15},{17,16},{18,... | collective-permute-start | bytes 3145736 | tf_op jit(solution)/shard_map/ppermute | solution.py:530
  385.6 42.6 %collective-permute-start.21 = (f32[128,2048]{1,0:T(8,128)S(1)}, f32[128,2048]{1,0:T(8,128)S(1)}, u32[]{:S(2)}, u32[]{:S(2)}) collective-permute-start(f32[128,2048]{1,0:T(8,128)S(1)} %get-tuple-element.282), channel_id=1, source_target_pairs={{0,1},{3,2},{4,5},{7,6},{8,9},{11,10},{12,13},{15,14},{16,17},{19,... | collective-permute-start | bytes 3145736 | tf_op jit(solution)/shard_map/ppermute | solution.py:530
  408.0 37.6 %collective-permute-start.25 = (f32[128,2048]{1,0:T(8,128)}, f32[128,2048]{1,0:T(8,128)}, u32[]{:S(2)}, u32[]{:S(2)}) collective-permute-start(f32[128,2048]{1,0:T(8,128)} %add.379), channel_id=1, source_target_pairs={{1,2},{2,1},{5,6},{6,5},{9,10},{10,9},{13,14},{14,13},{17,18},{18,... | collective-permute-start | bytes 3145736 | tf_op jit(solution)/shard_map/ppermute | solution.py:530
  409.8 42.4 %collective-permute-start.26 = (f32[128,2048]{1,0:T(8,128)}, f32[128,2048]{1,0:T(8,128)}, u32[]{:S(2)}, u32[]{:S(2)}) collective-permute-start(f32[128,2048]{1,0:T(8,128)} %add.380), channel_id=1, source_target_pairs={{1,0},{2,3},{5,4},{6,7},{9,8},{10,11},{13,12},{14,15},{17,16},{18,... | collective-permute-start | bytes 3145736 | tf_op jit(solution)/shard_map/ppermute | solution.py:530
  411.3 40.9 %collective-permute-start.24 = (f32[128,2048]{1,0:T(8,128)}, f32[128,2048]{1,0:T(8,128)}, u32[]{:S(2)}, u32[]{:S(2)}) collective-permute-start(f32[128,2048]{1,0:T(8,128)} %get-tuple-element.286), channel_id=1, source_target_pairs={{0,1},{3,2},{4,5},{7,6},{8,9},{11,10},{12,13},{15,14},{16,17},{19,... | collective-permute-start | bytes 3145736 | tf_op jit(solution)/shard_map/ppermute | solution.py:530
  457.2 38.0 %collective-permute-start.32 = (f32[128,2048]{1,0:T(8,128)S(1)}, f32[128,2048]{1,0:T(8,128)}, u32[]{:S(2)}, u32[]{:S(2)}) collective-permute-start(f32[128,2048]{1,0:T(8,128)S(1)} %add.386), channel_id=1, source_target_pairs={{1,0},{2,3},{5,4},{6,7},{9,8},{10,11},{13,12},{14,15},{17,16},{18,... | collective-permute-start | bytes 3145736 | tf_op jit(solution)/shard_map/ppermute | solution.py:530
  458.5 39.0 %collective-permute-start.30 = (f32[128,2048]{1,0:T(8,128)}, f32[128,2048]{1,0:T(8,128)}, u32[]{:S(2)}, u32[]{:S(2)}) collective-permute-start(f32[128,2048]{1,0:T(8,128)} %get-tuple-element.294), channel_id=1, source_target_pairs={{0,1},{3,2},{4,5},{7,6},{8,9},{11,10},{12,13},{15,14},{16,17},{19,... | collective-permute-start | bytes 3145736 | tf_op jit(solution)/shard_map/ppermute | solution.py:530
  481.3 52.8 %collective-permute-start.34 = (f32[128,2048]{1,0:T(8,128)}, f32[128,2048]{1,0:T(8,128)}, u32[]{:S(2)}, u32[]{:S(2)}) collective-permute-start(f32[128,2048]{1,0:T(8,128)} %add.388), channel_id=1, source_target_pairs={{1,2},{2,1},{5,6},{6,5},{9,10},{10,9},{13,14},{14,13},{17,18},{18,... | collective-permute-start | bytes 3145736 | tf_op jit(solution)/shard_map/ppermute | solution.py:530
  482.9 58.0 %collective-permute-start.35 = (f32[128,2048]{1,0:T(8,128)}, f32[128,2048]{1,0:T(8,128)}, u32[]{:S(2)}, u32[]{:S(2)}) collective-permute-start(f32[128,2048]{1,0:T(8,128)} %add.389), channel_id=1, source_target_pairs={{1,0},{2,3},{5,4},{6,7},{9,8},{10,11},{13,12},{14,15},{17,16},{18,... | collective-permute-start | bytes 3145736 | tf_op jit(solution)/shard_map/ppermute | solution.py:530
  484.2 56.7 %collective-permute-start.33 = (f32[128,2048]{1,0:T(8,128)}, f32[128,2048]{1,0:T(8,128)}, u32[]{:S(2)}, u32[]{:S(2)}) collective-permute-start(f32[128,2048]{1,0:T(8,128)} %get-tuple-element.298), channel_id=1, source_target_pairs={{0,1},{3,2},{4,5},{7,6},{8,9},{11,10},{12,13},{15,14},{16,17},{19,... | collective-permute-start | bytes 3145736 | tf_op jit(solution)/shard_map/ppermute | solution.py:530
  499.2 49.9 %collective-permute-start.38 = (f32[128,2048]{1,0:T(8,128)S(1)}, f32[128,2048]{1,0:T(8,128)}, u32[]{:S(2)}, u32[]{:S(2)}) collective-permute-start(f32[128,2048]{1,0:T(8,128)S(1)} %add.392), channel_id=1, source_target_pairs={{1,0},{2,3},{5,4},{6,7},{9,8},{10,11},{13,12},{14,15},{17,16},{18,... | collective-permute-start | bytes 3145736 | tf_op jit(solution)/shard_map/ppermute | solution.py:530
  549.1 37.2 %collective-permute-start.39 = (f32[128,2048]{1,0:T(8,128)}, f32[128,2048]{1,0:T(8,128)}, u32[]{:S(2)}, u32[]{:S(2)}) collective-permute-start(f32[128,2048]{1,0:T(8,128)} %get-tuple-element.308), channel_id=1, source_target_pairs={{0,1},{3,2},{4,5},{7,6},{8,9},{11,10},{12,13},{15,14},{16,17},{19,... | collective-permute-start | bytes 3145736 | tf_op jit(solution)/shard_map/ppermute | solution.py:530
  623.5 41.6 %collective-permute-start.49 = (f32[128,2048]{1,0:T(8,128)S(1)}, f32[128,2048]{1,0:T(8,128)S(1)}, u32[]{:S(2)}, u32[]{:S(2)}) collective-permute-start(f32[128,2048]{1,0:T(8,128)S(1)} %add.406), channel_id=1, source_target_pairs={{1,0},{2,3},{5,4},{6,7},{9,8},{10,11},{13,12},{14,15},{17,16},{18,... | collective-permute-start | bytes 3145736 | tf_op jit(solution)/shard_map/ppermute | solution.py:530
  644.2 39.0 %collective-permute-start.50 = (f32[40,2048]{1,0:T(8,128)S(1)}, f32[40,2048]{1,0:T(8,128)S(1)}, u32[]{:S(2)}, u32[]{:S(2)}) collective-permute-start(f32[40,2048]{1,0:T(8,128)S(1)} %add.408), channel_id=1, source_target_pairs={{1,0},{2,3},{5,4},{6,7},{9,8},{10,11},{13,12},{14,15},{17,16},{18,... | collective-permute-start | bytes 983048 | tf_op jit(solution)/shard_map/ppermute | solution.py:530
  (280 other events, 2406.3 us)
Sparse Core Ops, SparseCore 0:
  304.4 40.6 reduce-scatter.4
  349.2 71.2 reduce-scatter.10
  424.9 71.2 reduce-scatter.8
  500.1 71.2 reduce-scatter.6

commit v2 on v1

--- a/solution.py
+++ b/solution.py
@@ -13,6 +13,7 @@
 HEAD = 64
 STATE = 128
 PAIR = 2 * HEAD
+REST = 3 * STATE
 
 epsilon = 1e-05
 
@@ -77,12 +78,12 @@
     return result
 
 
-def chunk_terms(dt_ref, aux, head_ref, spread_ref):
+def chunk_terms(dt, aux, head_ref, spread_ref):
     row = lax.broadcasted_iota(jnp.int32, (CHUNK, CHUNK), 0)
     col = lax.broadcasted_iota(jnp.int32, (CHUNK, CHUNK), 1)
     lower = jnp.where(row >= col, 1.0, 0.0)
     upper = jnp.where(row <= col, 1.0, 0.0)
-    raw = dt_ref[...] + head_ref[0:1, :]
+    raw = dt + head_ref[0:1, :]
     step = softplus(raw)
     decay = step * head_ref[1:2, :]
     running = dot_exact(lower, decay)
@@ -112,16 +113,16 @@
 
 
 def forward_kernel(
-    x_ref, x_before, z_ref, bc_ref, bc_before, dt_ref, aux_ref, ids_ref,
-    chan_ref, taps_bc_ref, head_ref, spread_ref, start_ref,
-    y_ref, unit_ref, square_ref, states_ref, final_ref,
+    x_ref, x_before, z_ref, rest_ref, rest_before, aux_ref, ids_ref,
+    chan_ref, taps_bc_ref, head_ref, spread_ref, back_ref, start_ref,
+    scanned_ref, unit_ref, stats_ref, states_ref, final_ref,
     x_pad, bc_pad, memory, step_s, reach_s, tail_s,
 ):
     @pl.when(pl.program_id(0) == 0)
     def _():
         memory[...] = start_ref[...]
         x_pad[0:8, :] = x_before[...]
-        bc_pad[0:8, :] = bc_before[...]
+        bc_pad[0:8, :] = rest_before[:, : 2 * STATE]
 
     @pl.when(pl.program_id(0) > 0)
     def _():
@@ -130,12 +131,12 @@
 
     aux = aux_ref[...]
     x_pad[8:, :] = x_ref[...]
-    bc_pad[8:, :] = bc_ref[...]
+    bc_pad[8:, :] = rest_ref[:, : 2 * STATE]
     pre_bc = conv_rows(bc_pad, slice(None), taps_bc_ref[...], aux)
     bc = pre_bc * sigmoid(pre_bc)
     b_rows, c_rows = bc[:, :STATE], bc[:, STATE:]
     _, _, _, running, running_t, _, step_e, reach_e, tail_e, kept_e = chunk_terms(
-        dt_ref, aux, head_ref, spread_ref
+        rest_ref[:, 2 * STATE : 2 * STATE + head_ref.shape[1]], aux, head_ref, spread_ref
     )
     step_s[...] = step_e
     reach_s[...] = reach_e
@@ -146,6 +147,7 @@
     scores = jnp.where(linked, mm("scores", c_rows, b_rows, ((1,), (1,))), 0.0)
     first, second = pair_masks()
     squares = jnp.zeros((CHUNK, 1), f32)
+    share = jnp.zeros((CHUNK, 1), f32)
     for pair in range(x_ref.shape[1] // PAIR):
         lanes = slice(pair * PAIR, (pair + 1) * PAIR)
         chan = chan_ref[:, lanes]
@@ -164,21 +166,25 @@
         memory[:, lanes] = kept_e[:, lanes] * old + mm(
             "state", b_rows, tail_s[:, lanes] * u, ((0,), (0,))
         )
-        y_ref[:, lanes] = y
+        scanned = y + chan[5:6] * x_conv
+        scanned_ref[:, lanes] = scanned
         z = z_ref[:, lanes]
-        gated = (y + chan[5:6] * x_conv) * (z * sigmoid(z))
-        unit_ref[:, lanes] = (gated * chan[6:7]).astype(bf16)
+        gated = scanned * (z * sigmoid(z))
+        unit = (gated * chan[6:7]).astype(bf16)
+        unit_ref[:, lanes] = unit
         squares = squares + jnp.sum(gated * gated, 1, keepdims=True)
-    square_ref[...] = squares
+        share = share + jnp.sum(unit.astype(f32) * back_ref[:, lanes], 1, keepdims=True)
+    stats_ref[:, 0:1] = squares
+    stats_ref[:, 1:2] = share
     final_ref[...] = memory[...]
 
 
 def backward_kernel(
-    x_ref, x_before, z_ref, bc_ref, bc_before, dt_ref, aux_ref, ids_ref,
+    x_ref, x_before, z_ref, rest_ref, rest_before, aux_ref, ids_ref,
     chan_ref, taps_bc_ref, head_ref, spread_ref,
-    x_within, bc_within, gather_ref, y_ref, state_ref, next_ref, d_unit_ref, coef_ref,
+    x_within, rest_within, gather_ref, scanned_ref, state_ref, next_ref, back_ref, factors_ref,
     d_memory_in, dconv_in, dconv_bc_in, g_chan_in, g_bc_in, g_head_in,
-    dz_ref, dx_ref, dbc_ref, ddt_ref,
+    dz_ref, dx_ref, drest_ref,
     d_memory, dconv_ref, dconv_bc_ref, g_chan_ref, g_bc_ref, g_head_ref,
     x_pad, bc_pad, step_s, reach_s, tail_s, dconv_pad, dconv_bc_pad, step_grad_s, run_grad_s, later,
 ):
@@ -198,16 +204,16 @@
     @pl.when(index == count - 1)
     def _():
         x_pad[0:8, :] = x_before[...]
-        bc_pad[0:8, :] = bc_before[...]
+        bc_pad[0:8, :] = rest_before[:, : 2 * STATE]
 
     @pl.when(index < count - 1)
     def _():
         x_pad[0:8, :] = x_within[...]
-        bc_pad[0:8, :] = bc_within[...]
+        bc_pad[0:8, :] = rest_within[:, : 2 * STATE]
 
     aux = aux_ref[...]
     x_pad[8:, :] = x_ref[...]
-    bc_pad[8:, :] = bc_ref[...]
+    bc_pad[8:, :] = rest_ref[:, : 2 * STATE]
     dconv_pad[CHUNK:, :] = dconv_pad[0:8, :]
     dconv_bc_pad[CHUNK:, :] = dconv_bc_pad[0:8, :]
     taps_bc = taps_bc_ref[...]
@@ -216,7 +222,7 @@
     bc = pre_bc * sig_bc
     b_rows, c_rows = bc[:, :STATE], bc[:, STATE:]
     raw, step, decay, running, running_t, upper, step_e, reach_e, tail_e, kept_e = chunk_terms(
-        dt_ref, aux, head_ref, spread_ref
+        rest_ref[:, 2 * STATE : 2 * STATE + head_ref.shape[1]], aux, head_ref, spread_ref
     )
     step_s[...] = step_e
     reach_s[...] = reach_e
@@ -226,7 +232,8 @@
     linked = (row <= col) & (aux[:, 9:10] == ids_ref[...])
     scores_t = jnp.where(linked, mm("scores", b_rows, c_rows, ((1,), (1,))), 0.0)
     first, second = pair_masks()
-    coef = coef_ref[...]
+    scale = factors_ref[:, 0:1]
+    coef = factors_ref[:, 1:2]
     d_scores_t = jnp.zeros((CHUNK, CHUNK), f32)
     d_b = jnp.zeros((CHUNK, STATE), f32)
     d_c = jnp.zeros((CHUNK, STATE), f32)
@@ -241,10 +248,10 @@
         z = z_ref[:, lanes]
         sig_z = sigmoid(z)
         silu_z = z * sig_z
-        y = y_ref[:, lanes]
-        scanned = y + chan[5:6] * x_conv
+        scanned = scanned_ref[:, lanes]
+        y = scanned - chan[5:6] * x_conv
         gated = scanned * silu_z
-        d_unit = d_unit_ref[:, lanes]
+        d_unit = scale * back_ref[:, lanes]
         d_gated = d_unit * chan[6:7] - coef * gated
         dz_ref[:, lanes] = (d_gated * scanned * (sig_z + silu_z * (1.0 - sig_z))).astype(bf16)
         dy = d_gated * silu_z
@@ -293,7 +300,8 @@
     d_decay = dot_exact(upper, run_grad_s[...]) + ends[0:1]
     d_step = step_grad_s[...] + head_ref[1:2, :] * d_decay
     d_raw = d_step * sigmoid(raw)
-    ddt_ref[...] = d_raw.astype(bf16)
+    drest_ref[:, 2 * STATE :] = jnp.zeros((CHUNK, REST - 2 * STATE), bf16)
+    drest_ref[:, 2 * STATE : 2 * STATE + heads] = d_raw.astype(bf16)
     g_head_ref[0:1, :] += jnp.sum(d_raw, 0, keepdims=True)
     g_head_ref[1:2, :] += jnp.sum(d_decay * decay, 0, keepdims=True)
 
@@ -303,14 +311,14 @@
     d_conv = jnp.concatenate([d_b, d_c], 1) * (sig_bc + pre_bc * sig_bc * (1.0 - sig_bc))
     dconv_bc_pad[0:CHUNK, :] = d_conv
     d_pre = taps_bc[0:1] * d_conv
-    g_bc_ref[0:1, :] += jnp.sum(d_conv * bc_ref[...], 0, keepdims=True)
+    g_bc_ref[0:1, :] += jnp.sum(d_conv * rest_ref[:, : 2 * STATE], 0, keepdims=True)
     for offset in range(1, 4):
         ahead = dconv_bc_pad[pl.ds(offset, CHUNK), :] * aux[:, 2 + offset : 3 + offset]
         d_pre = d_pre + taps_bc[offset : offset + 1] * ahead
         behind = bc_pad[pl.ds(8 - offset, CHUNK), :] * aux[:, offset - 1 : offset]
         g_bc_ref[offset : offset + 1, :] += jnp.sum(d_conv * behind, 0, keepdims=True)
     g_bc_ref[4:5, :] += jnp.sum(d_conv, 0, keepdims=True)
-    dbc_ref[...] = d_pre.astype(bf16)
+    drest_ref[:, : 2 * STATE] = d_pre.astype(bf16)
     dconv_ref[...] = dconv_pad[0:8, :]
     dconv_bc_ref[...] = dconv_bc_pad[0:8, :]
 
@@ -323,25 +331,22 @@
     return pl.BlockSpec((8, width), lambda i: (jnp.maximum(place(i) * (CHUNK // 8) - 1, 0), 0))
 
 
-def last_rows_spec(array):
-    last = array.shape[0] // 8 - 1
-    return pl.BlockSpec((8, array.shape[1]), lambda i: (last, 0))
+def fixed_rows_spec(width, block):
+    return pl.BlockSpec((8, width), lambda i: (block, 0))
 
 
 def whole_spec(shape):
     return pl.BlockSpec(shape, lambda i: (0,) * len(shape))
 
 
-def sequence_specs(segment, place, first_chunk):
-    x, x_before, _, _, bc_before, dt = segment[:6]
-    inner, heads = x.shape[1], dt.shape[1]
+def sequence_specs(segment, place, first_chunk, before):
+    inner, heads = segment[0].shape[1], segment[-1].shape[0]
     return [
         rows_spec(inner, place),
-        last_rows_spec(x_before),
+        fixed_rows_spec(inner, before),
         rows_spec(inner, place),
-        rows_spec(2 * STATE, place),
-        last_rows_spec(bc_before),
-        rows_spec(heads, place),
+        rows_spec(REST, place),
+        fixed_rows_spec(REST, before),
         rows_spec(16, lambda i: place(i) + first_chunk),
         pl.BlockSpec((1, CHUNK), lambda i: (0, place(i) + first_chunk)),
         whole_spec((8, inner)),
@@ -351,7 +356,7 @@
     ]
 
 
-def forward_scan(segment, start, first_chunk):
+def forward_scan(segment, back, start, first_chunk):
     tokens, inner = segment[0].shape
     chunks = tokens // CHUNK
 
@@ -361,18 +366,19 @@
     return pl.pallas_call(
         forward_kernel,
         grid=(chunks,),
-        in_specs=sequence_specs(segment, place, first_chunk) + [whole_spec((STATE, inner))],
+        in_specs=sequence_specs(segment, place, first_chunk, segment[1].shape[0] // 8 - 1)
+        + [rows_spec(inner, place), whole_spec((STATE, inner))],
         out_specs=[
             rows_spec(inner, place),
             rows_spec(inner, place),
-            rows_spec(1, place),
+            rows_spec(2, place),
             pl.BlockSpec((1, STATE, inner), lambda i: (i, 0, 0)),
             whole_spec((STATE, inner)),
         ],
         out_shape=[
             jax.ShapeDtypeStruct((tokens, inner), f32),
             jax.ShapeDtypeStruct((tokens, inner), bf16),
-            jax.ShapeDtypeStruct((tokens, 1), f32),
+            jax.ShapeDtypeStruct((tokens, 2), f32),
             jax.ShapeDtypeStruct((chunks, STATE, inner), STATE_TYPE),
             jax.ShapeDtypeStruct((STATE, inner), f32),
         ],
@@ -384,50 +390,53 @@
             pltpu.VMEM((CHUNK, inner), f32),
             pltpu.VMEM((CHUNK, inner), f32),
         ],
-        compiler_params=pltpu.CompilerParams(vmem_limit_bytes=32 << 20),
+        compiler_params=pltpu.CompilerParams(vmem_limit_bytes=24 << 20),
         cost_estimate=pl.CostEstimate(
-            flops=tokens * inner * 2000, bytes_accessed=tokens * inner * 18, transcendentals=0
+            flops=0, bytes_accessed=0, transcendentals=0
         ),
         name="forward_scan",
-    )(*segment, start)
-
-
-def backward_scan(segment, first_chunk, gather, y, states, next_states, d_unit, coef, carried):
-    tokens, inner = segment[0].shape
-    heads = segment[5].shape[1]
+    )(*segment, back, start)
+
+
+def backward_scan(
+    segment, first_chunk, offset, tokens, gather, scanned, states, next_states, next_at, back, factors,
+    carried,
+):
+    inner, heads = segment[0].shape[1], segment[-1].shape[0]
     chunks = tokens // CHUNK
+    x_before, rest_before, before = segment[1], segment[4], segment[1].shape[0] // 8 - 1
+    if offset:
+        x_before, rest_before, before = segment[0], segment[3], offset * (CHUNK // 8) - 1
+    segment = (segment[0], x_before, segment[2], segment[3], rest_before) + tuple(segment[5:])
 
     def place(i):
+        return offset + chunks - 1 - i
+
+    def own(i):
         return chunks - 1 - i
 
     carried_specs = [whole_spec(array.shape) for array in carried]
     return pl.pallas_call(
         backward_kernel,
         grid=(chunks,),
-        in_specs=sequence_specs(segment, place, first_chunk)
+        in_specs=sequence_specs(segment, place, first_chunk, before)
         + [
             within_spec(inner, place),
-            within_spec(2 * STATE, place),
+            within_spec(REST, place),
             whole_spec((inner, heads)),
             rows_spec(inner, place),
             pl.BlockSpec((1, STATE, inner), lambda i: (place(i), 0, 0)),
-            pl.BlockSpec((1, STATE, inner), lambda i: (0, 0, 0)),
+            pl.BlockSpec((1, STATE, inner), lambda i: (next_at, 0, 0)),
             rows_spec(inner, place),
-            rows_spec(1, place),
+            rows_spec(3, lambda i: place(i) + first_chunk),
         ]
         + carried_specs,
-        out_specs=[
-            rows_spec(inner, place),
-            rows_spec(inner, place),
-            rows_spec(2 * STATE, place),
-            rows_spec(heads, place),
-        ]
+        out_specs=[rows_spec(inner, own), rows_spec(inner, own), rows_spec(REST, own)]
         + carried_specs,
         out_shape=[
             jax.ShapeDtypeStruct((tokens, inner), bf16),
             jax.ShapeDtypeStruct((tokens, inner), bf16),
-            jax.ShapeDtypeStruct((tokens, 2 * STATE), bf16),
-            jax.ShapeDtypeStruct((tokens, heads), bf16),
+            jax.ShapeDtypeStruct((tokens, REST), bf16),
         ]
         + [jax.ShapeDtypeStruct(array.shape, f32) for array in carried],
         scratch_shapes=[
@@ -442,12 +451,14 @@
             pltpu.VMEM((CHUNK, heads), f32),
             pltpu.VMEM((STATE, inner), STATE_TYPE),
         ],
-        compiler_params=pltpu.CompilerParams(vmem_limit_bytes=32 << 20),
+        compiler_params=pltpu.CompilerParams(vmem_limit_bytes=56 << 20),
         cost_estimate=pl.CostEstimate(
-            flops=tokens * inner * 4000, bytes_accessed=tokens * inner * 26, transcendentals=0
+            flops=0, bytes_accessed=0, transcendentals=0
         ),
         name="backward_scan",
-    )(*segment, segment[0], segment[3], gather, y, states, next_states, d_unit, coef, *carried)
+    )(
+        *segment, segment[0], segment[3], gather, scanned, states, next_states, back, factors, *carried
+    )
 
 
 def backward_start(inner, heads):
@@ -455,6 +466,50 @@
         jnp.zeros(shape, f32)
         for shape in [(STATE, inner), (8, inner), (8, 2 * STATE), (8, inner), (8, 2 * STATE), (8, heads)]
     ]
+
+
+def normed_kernel(
+    d_z, d_x, d_rest, z_weight, x_weight, rest_weight, hidden, factors, part_ref, norm_grad_ref
+):
+    part = (
+        dot(d_z[...], z_weight[...], ((1,), (1,)))
+        + dot(d_x[...], x_weight[...], ((1,), (1,)))
+        + dot(d_rest[...], rest_weight[...], ((1,), (1,)))
+    )
+    part_ref[...] = part
+    hat = hidden[...].astype(f32) * factors[:, 2:3]
+    norm_grad_ref[...] = jnp.broadcast_to(jnp.sum(part * hat, 0, keepdims=True), norm_grad_ref.shape)
+
+
+def normed_gradient(d_z, d_x, d_rest, z_weight, x_weight, rest_weight, hidden, factors, begin):
+    tokens, inner = d_z.shape
+    width = hidden.shape[1]
+    tile = 256
+    return pl.pallas_call(
+        normed_kernel,
+        grid=(width // tile,),
+        in_specs=[
+            whole_spec((tokens, inner)),
+            whole_spec((tokens, inner)),
+            whole_spec((tokens, REST)),
+            pl.BlockSpec((tile, inner), lambda i: (i, 0)),
+            pl.BlockSpec((tile, inner), lambda i: (i, 0)),
+            pl.BlockSpec((tile, REST), lambda i: (i, 0)),
+            pl.BlockSpec((tokens, tile), lambda i: (begin // tokens, i)),
+            pl.BlockSpec((tokens, 3), lambda i: (begin // tokens, 0)),
+        ],
+        out_specs=[
+            pl.BlockSpec((tokens, tile), lambda i: (0, i)),
+            pl.BlockSpec((8, tile), lambda i: (0, i)),
+        ],
+        out_shape=[
+            jax.ShapeDtypeStruct((tokens, width), f32),
+            jax.ShapeDtypeStruct((8, width), f32),
+        ],
+        compiler_params=pltpu.CompilerParams(vmem_limit_bytes=56 << 20),
+        cost_estimate=pl.CostEstimate(flops=0, bytes_accessed=0, transcendentals=0),
+        name="normed_gradient",
+    )(d_z, d_x, d_rest, z_weight, x_weight, rest_weight, hidden, factors)
 
 
 def token_masks(segment_ids):
@@ -497,45 +552,104 @@
 
 
 class LineSum:
-    def __init__(self, chains):
+    def __init__(self):
         me = lax.axis_index("tensor")
         self.outer = (me == 0) | (me == 3)
-        self.waiting = []
-        self.chains = [[None, None, None] for _ in range(chains)]
-        self.sent = [[None, None, None] for _ in range(chains)]
-        self.names = [[None, None, None] for _ in range(chains)]
-        self.next = 0
-        self.results = {}
+        self.waiting, self.flying, self.landed, self.unfinished = [], [], [], []
+        self.finish = None
 
     def add(self, name, piece):
         self.waiting.append((name, piece))
 
     def busy(self):
-        return bool(self.waiting) or any(part is not None for chain in self.chains for part in chain)
+        return bool(self.waiting or self.flying or self.landed)
+
+    def sums(self, pieces):
+        return [(name, jnp.where(self.outer, got, own)) for name, own, got in pieces]
+
+    def start_finishing(self, finish, after):
+        names = [name for name, _, _ in self.unfinished]
+        parts, after = lax.optimization_barrier(([part[1:] for part in self.unfinished], after))
+        self.unfinished = [(name,) + tuple(part) for name, part in zip(names, parts)]
+        self.finish = finish
+        return after
+
+    def arrive(self, got):
+        for (kind, name, own, inside), moved in zip(self.flying, got):
+            if kind == "both":
+                self.landed.append(("in",) + inside + (moved,))
+                self.landed.append(("out", name, own, moved))
+            else:
+                self.landed.append((kind, name, own, moved))
+        self.flying = []
 
     def turn(self, carried=()):
-        chain = self.next
-        self.next = (chain + 1) % len(self.chains)
-        held, sent, names = self.chains[chain], self.sent[chain], self.names[chain]
-        name, piece = self.waiting.pop(0) if self.waiting else (None, None)
-        tied = lax.optimization_barrier((tuple(sent), piece, tuple(carried)))
-        sent, piece, carried = tied
-        inward = None if held[0] is None else held[0] + sent[0]
-        across = None if held[1] is None else held[1] + sent[1]
-        if held[2] is not None:
-            self.results[names[2]] = jnp.where(self.outer, sent[2], held[2])
-        self.chains[chain] = [piece, inward, across]
-        self.names[chain] = [name, names[0], names[1]]
-        self.sent[chain] = [
-            None if part is None else lax.ppermute(part, "tensor", route)
-            for part, route in zip(self.chains[chain], (INWARD, ACROSS, OUTWARD))
-        ]
+        changed = {}
+        if self.finish is not None:
+            changed = self.finish(self.sums(self.unfinished[:4]))
+            self.unfinished = self.unfinished[4:]
+        got, changed, carried = lax.optimization_barrier(
+            ([flight[1] for flight in self.flying], changed, tuple(carried))
+        )
+        if changed:
+            self.finish.whole.update(changed)
+        self.flying = [flight[0] for flight in self.flying]
+        self.arrive(got)
+        send = []
+        fresh = self.waiting.pop(0) if self.waiting else None
+        beside = self.waiting.pop(0) if self.waiting and self.waiting[0][0][0] == "extra" else None
+        for kind, name, own, got in self.landed:
+            if kind == "in":
+                send.append(("across", name, own + got, None))
+            elif kind == "out":
+                self.unfinished.append((name, own, got))
+            elif fresh is not None and fresh[1].shape == own.shape:
+                joint = jnp.where(self.outer, fresh[1], own + got)
+                send.insert(0, ("both", name, joint, fresh))
+                fresh = None
+            else:
+                send.append(("out", name, own + got, None))
+        for piece in (beside, fresh):
+            if piece is not None:
+                send.insert(0, ("in", piece[0], piece[1], None))
+        self.landed = []
+        ready, carried = lax.optimization_barrier(([part[2] for part in send], tuple(carried)))
+        routes = {"both": INWARD + OUTWARD, "in": INWARD, "across": ACROSS, "out": OUTWARD}
+        for (kind, name, _, inside), part in zip(send, ready):
+            moved = lax.ppermute(part, "tensor", routes[kind])
+            self.flying.append(((kind, name, part, inside), moved))
         return carried
 
 
+class Finish:
+    def __init__(self, base, cot, norm_gain, rms, scale):
+        self.base, self.cot, self.norm_gain, self.rms, self.scale = base, cot, norm_gain, rms, scale
+        self.whole = {kind: jnp.zeros(base.shape, f32) for kind in ("out", "in")}
+
+    def __call__(self, pieces):
+        changed = []
+        for (kind, at, size), value in pieces:
+            if kind == "extra":
+                self.whole[kind] = value
+            else:
+                base = self.base[at : at + size].astype(f32)
+                if kind == "out":
+                    result = base + self.scale[at : at + size] * value
+                else:
+                    inverse = self.rms[at : at + size]
+                    hat = base * inverse
+                    d_hat = value * self.norm_gain[None, :]
+                    result = self.cot[at : at + size].astype(f32) + inverse * (
+                        d_hat - hat * jnp.mean(d_hat * hat, -1, keepdims=True)
+                    )
+                self.whole[kind] = lax.dynamic_update_slice(self.whole[kind], result, (at, 0))
+            changed.append(kind)
+        return {kind: self.whole[kind] for kind in sorted(set(changed))}
+
+
 SEGMENT = 256
-PIECE = 128
-CHAINS = 2
+PIECES = (256,)
+LAST_PIECES = (128, 128)
 
 
 def shards(
@@ -563,7 +677,7 @@
     inner = heads * HEAD
     count = tokens // SEGMENT
     chunks = SEGMENT // CHUNK
-    line = LineSum(CHAINS)
+    line = LineSum()
 
     rate = -jnp.exp(a_log)
     zero_row = jnp.zeros((1, inner), f32)
@@ -575,116 +689,113 @@
     owner = jnp.arange(inner, dtype=jnp.int32) // HEAD
     spread = (jnp.arange(heads, dtype=jnp.int32)[:, None] == owner[None, :]).astype(bf16)
     gather = (owner[:, None] == jnp.arange(heads, dtype=jnp.int32)[None, :]).astype(bf16)
+    rest_weight = jnp.concatenate(
+        [bc_weight, dt_weight, jnp.zeros((width, REST - 2 * STATE - heads), bf16)], 1
+    )
     shared = (
         token_masks(segment_ids), segment_ids.astype(f32)[None], chan, taps_bc, head_rows, spread,
     )
 
-    def rows(array, index):
-        return lax.slice_in_dim(array, index * SEGMENT, (index + 1) * SEGMENT, axis=0)
-
-    def split(array):
-        return [array[at : at + PIECE] for at in range(0, SEGMENT, PIECE)]
+    def pieces(kind, begin, array, sizes):
+        at = 0
+        for size in sizes:
+            line.add((kind, begin + at, size), rows(array, at, at + size))
+            at += size
+
+    def rows(array, begin, end):
+        return lax.slice_in_dim(array, begin, end, axis=0)
 
     memory = jnp.zeros((STATE, inner), f32)
-    segments, normed, hats, rms, ys, units, states, stats = [], [], [], [], [], [], [], []
-    for index in range(count):
-        hidden = rows(hidden_in, index)
-        if index:
-            memory, hidden = line.turn((memory, hidden))
-        base = hidden.astype(f32)
+    bounds = [(at, at + SEGMENT) for at in range(0, tokens, SEGMENT)]
+    count = len(bounds)
+    backs = []
+    gain = norm_gain
+    segments, normed, rms, scans, units, states, stats = [], [], [], [], [], [], []
+    for index, (begin, end) in enumerate(bounds):
+        base = rows(hidden_in, begin, end).astype(f32)
         rms.append(lax.rsqrt(jnp.mean(base * base, -1, keepdims=True) + epsilon))
-        normed.append((base * rms[-1] * norm_gain[None, :]).astype(bf16))
+        normed.append((base * rms[-1] * gain[None, :]).astype(bf16))
         x_pre = dot(normed[-1], x_weight)
-        bc_pre = dot(normed[-1], bc_weight)
+        rest_pre = dot(normed[-1], rest_weight)
         z_pre = dot(normed[-1], z_weight)
-        dt_pre = dot(normed[-1], dt_weight)
-        before = segments[-1] if segments else (x_pre, None, None, bc_pre)
-        segments.append((x_pre, before[0], z_pre, bc_pre, before[3], dt_pre) + shared)
-        y, unit, squares, state, memory = forward_scan(segments[-1], memory, index * chunks)
-        proj = dot(unit, out_weight)
-        for number, piece in enumerate(split(proj)):
-            line.add(("out", index * SEGMENT + number * PIECE), piece)
-        share = jnp.sum(rows(cotangent, index).astype(f32) * proj, -1)
-        stats.append(jnp.concatenate([squares.T, share[None]], 0))
-        ys.append(y)
+        backs.append(contract_cols(rows(cotangent, begin, end), out_weight))
+        before = segments[-1] if segments else (x_pre, None, None, rest_pre)
+        segments.append((x_pre, before[0], z_pre, rest_pre, before[3]) + shared)
+        scanned, unit, stat, state, memory = forward_scan(
+            segments[-1], backs[-1], memory, begin // CHUNK
+        )
+        piece = dot(unit, out_weight)
+        pieces("out", begin, piece, PIECES)
+        if index in (0, 2):
+            memory, gain = line.turn((memory, gain))
+        stats.append(stat)
+        scans.append(scanned)
         units.append(unit)
         states.append(state)
 
-    (local,) = line.turn((jnp.concatenate(stats, 1),))
-    total = lax.psum(local, "tensor")
+    rms_all = jnp.concatenate(rms, 0)
+    total = lax.psum(jnp.concatenate(stats, 0), "tensor")
     (total,) = line.turn((total,))
-    scale = lax.rsqrt(total[0] / D_INNER + epsilon)[:, None]
-    d_scale = total[1][:, None]
-    coef = d_scale * scale * scale * scale / D_INNER
-    d_proj = (scale * cotangent.astype(f32)).astype(bf16)
+    scale = lax.rsqrt(total[:, 0:1] / D_INNER + epsilon)
+    coef = total[:, 1:2] * scale * scale * scale / D_INNER
+    factors = jnp.concatenate([scale, coef, rms_all], 1)
+    normed_all = jnp.concatenate(normed, 0)
+    units_all = jnp.concatenate(units, 0)
 
     carried = backward_start(inner, heads)
-    grads = [None] * count
-    norm_grad = jnp.zeros((width,), f32)
+    grads = []
+    norm_grad = jnp.zeros((8, width), f32)
     for index in reversed(range(count)):
-        d_unit = contract_cols(rows(d_proj, index), out_weight)
-        outs = backward_scan(
-            segments[index], index * chunks, gather, ys[index], states[index],
-            states[min(index + 1, count - 1)], d_unit, rows(coef, index), carried,
+        begin, end = bounds[index]
+        d_z, d_x, d_rest, *carried = backward_scan(
+            segments[index], begin // CHUNK, 0, SEGMENT, gather, scans[index],
+            states[index], states[min(index + 1, count - 1)], 0, backs[index], factors, carried,
         )
-        d_z, d_x, d_bc, d_dt = grads[index] = outs[:4]
-        carried = outs[4:]
-        part = (
-            contract_cols(d_z, z_weight)
-            + contract_cols(d_x, x_weight)
-            + contract_cols(d_dt, dt_weight)
-            + contract_cols(d_bc, bc_weight)
+        grads.append((d_z, d_x, d_rest))
+        part, share = normed_gradient(
+            d_z, d_x, d_rest, z_weight, x_weight, rest_weight, hidden_in, factors, begin
         )
-        base = rows(hidden_in, index).astype(f32)
-        norm_grad = norm_grad + jnp.sum(part * (base * rms[index]), 0)
-        for number, piece in reversed(list(enumerate(split(part)))):
-            line.add(("in", index * SEGMENT + number * PIECE), piece)
-        *carried, norm_grad = line.turn(tuple(carried) + (norm_grad,))
-
-    normed_all = jnp.concatenate(normed, 0)
-    unit_all = jnp.concatenate(units, 0)
-    d_z, d_x, d_bc, d_dt = [jnp.concatenate([g[k] for g in grads], 0) for k in range(4)]
-    d_rest = jnp.concatenate([d_bc, d_dt], 1)
-    rest_share = lax.psum_scatter(
-        contract_rows(normed_all, d_rest), "dp", scatter_dimension=0, tiled=True
-    )
-    out_share = lax.psum_scatter(
-        contract_rows(unit_all, d_proj), "dp", scatter_dimension=1, tiled=True
-    )
-    z_share = lax.psum_scatter(contract_rows(normed_all, d_z), "dp", scatter_dimension=0, tiled=True)
-    x_share = lax.psum_scatter(contract_rows(normed_all, d_x), "dp", scatter_dimension=0, tiled=True)
-    norm_grad, g_chan, g_bc, g_head = lax.psum((norm_grad,) + tuple(carried[3:]), "dp")
+        norm_grad = norm_grad + share
+        pieces("in", begin, part, PIECES if begin else LAST_PIECES)
+        if index == count - 1:
+            d_proj = (scale * cotangent.astype(f32)).astype(bf16)
+            out_grad = contract_rows(units_all, d_proj)
+            *carried, norm_grad, out_grad = line.turn((*carried, norm_grad, out_grad))
+            out_share = lax.psum_scatter(out_grad, "dp", scatter_dimension=1, tiled=True)
+        else:
+            *carried, norm_grad = line.turn((*carried, norm_grad))
+
+    d_z, d_x, d_rest = [jnp.concatenate([g[k] for g in reversed(grads)], 0) for k in range(3)]
+    d_z, d_rest, out_share = lax.optimization_barrier((d_z, d_rest, out_share))
+    rest_grad = contract_rows(normed_all, d_rest)
+    z_grad = contract_rows(normed_all, d_z)
+    rest_share = lax.psum_scatter(rest_grad, "dp", scatter_dimension=0, tiled=True)
+    z_grad, d_x, rest_share, *carried = line.turn((z_grad, d_x, rest_share, *carried))
+    z_share = lax.psum_scatter(z_grad, "dp", scatter_dimension=0, tiled=True)
+    norm_grad, g_chan, g_bc, g_head = lax.psum((norm_grad[0], *carried[3:]), "dp")
+    x_grad = contract_rows(normed_all, d_x)
+    x_grad, norm_grad = line.turn((x_grad, norm_grad))
+    x_grad, z_share = lax.optimization_barrier((x_grad, z_share))
+    x_share = lax.psum_scatter(x_grad, "dp", scatter_dimension=0, tiled=True)
 
     bc_part = rest_share[:, : 2 * STATE]
     extra = jnp.concatenate([norm_grad, g_bc.reshape(-1), bc_part.reshape(-1)])
     extra_rows = -(-extra.shape[0] // (8 * width)) * 8
     extra = jnp.pad(extra, (0, extra_rows * width - extra.shape[0])).reshape(extra_rows, width)
-    line.add(("extra", 0), extra)
-
-    output = jnp.zeros((tokens, width), f32)
-    input_grad = jnp.zeros((tokens, width), f32)
-    done = 0
+    extra = line.start_finishing(
+        Finish(hidden_in, cotangent, norm_gain, rms_all, scale), extra
+    )
+    line.add(("extra", 0, extra_rows), extra)
+
     while line.busy():
         line.turn()
-    for (kind, at), value in line.results.items():
-        if kind == "extra":
-            flat = value.reshape(-1)
-            norm_gain_grad = flat[:width]
-            g_bc = flat[width : width + g_bc.size].reshape(g_bc.shape)
-            begin = width + g_bc.size
-            bc_share = flat[begin : begin + bc_part.size].reshape(bc_part.shape)
-            continue
-        base = hidden_in[at : at + PIECE].astype(f32)
-        if kind == "out":
-            result = base + scale[at : at + PIECE] * value
-            output = lax.dynamic_update_slice(output, result, (at, 0))
-        else:
-            cot = cotangent[at : at + PIECE].astype(f32)
-            inverse = rms[at // SEGMENT][at % SEGMENT : at % SEGMENT + PIECE]
-            hat = base * inverse
-            d_hat = value * norm_gain[None, :]
-            result = cot + inverse * (d_hat - hat * jnp.mean(d_hat * hat, -1, keepdims=True))
-            input_grad = lax.dynamic_update_slice(input_grad, result, (at, 0))
+    line.finish.whole.update(line.finish(line.sums(line.unfinished)))
+    output, input_grad = line.finish.whole["out"], line.finish.whole["in"]
+    flat = line.finish.whole["extra"].reshape(-1)
+    norm_gain_grad = flat[:width]
+    g_bc = flat[width : width + g_bc.size].reshape(g_bc.shape)
+    begin = width + g_bc.size
+    bc_share = flat[begin : begin + bc_part.size].reshape(bc_part.shape)
     return (
         output,
         input_grad,
@@ -692,7 +803,7 @@
         z_share,
         x_share,
         bc_share,
-        rest_share[:, 2 * STATE :],
+        rest_share[:, 2 * STATE : 2 * STATE + heads],
         g_chan[:4],
         g_chan[4],
         g_bc[:4],

time: 702 us -> 645 us (0.919)
  starting transfers between devices: 194 us -> 60.3 us
  waiting for transfers between devices: 60.6 us -> 151 us
  Pallas kernels: 66 us -> 119 us
  matrix products: 112 us -> 76.6 us
  local copies, waits for them, and re-layouts: 84.4 us -> 59.6 us
  other arithmetic: 107 us -> 97.4 us
    ppermute x51 -> x25, starting transfers between devices: 193 us -> 60.1 us  [turn(): moved = lax.ppermute(part, 'tensor', routes[kind])]
    ppermute x51 -> x25, waiting for transfers between devices: 60.6 us -> 130 us  [turn(): moved = lax.ppermute(part, 'tensor', routes[kind])]
    pallas_call x0 -> x4, Pallas kernels: none -> 40.4 us  [normed_gradient(): pl.pallas_call(normed_kernel, grid=(width // tile,), in_specs=[whole_spec...]
    dot_general x44 -> x24, matrix products: 112 us -> 76.6 us  [dot(): lax.dot_general(left, right, (dims, ((), ())), preferred_element_type=f32)]
    reduce_scatter x4, waiting for transfers between devices: 0.01 us -> 21.1 us  [the longest x1 21.1 us: shards(): z_share = lax.psum_scatter(z_grad, 'dp', scatter_dimension=0, tiled=True)]
    slice x18 -> x5, local copies, waits for them, and re-layouts: 25.3 us -> 4.29 us  [the longest x1 1.57 us: shards(): rest_share[:, 2 * STATE:2 * STATE + heads]]
    add x38 -> x20, other arithmetic: 63.4 us -> 42.8 us  [the longest x10 24.9 us: turn(): send.append(('across', name, own + got, None))]
    select_n x1 -> x6, other arithmetic: 0.04 us -> 18.8 us  [the longest x5 18.7 us: turn(): joint = jnp.where(self.outer, fresh[1], own + got)]
  transfers between devices with their start and end apart: 55 -> 29, of which waited for: 10 -> 12; matrix products, arithmetic and copies ran while one was open for 34% -> 24% of each run, Pallas kernels for 7% -> 18%
where the time goes in v2:
time: 645 us; the launch traced here: 635 us
  waiting for transfers between devices  151 us (23%)
  Pallas kernels  119 us (18%)
  other arithmetic  97.4 us (15%)
  matrix products  76.6 us (12%)
  starting transfers between devices  60.3 us (9%)
  local copies, waits for them, and re-layouts  59.6 us (9%)
  blocking collectives  56.1 us (9%)
  between operations  15.7 us (2%)
    ppermute x25, waiting for transfers between devices, turn(): moved = lax.ppermute(part, 'tensor', routes[kind])  130 us
    dot_general x24, matrix products, dot(): lax.dot_general(left, right, (dims, ((), ())), preferred_element_type=f32)  76.6 us
    ppermute x25, starting transfers between devices, turn(): moved = lax.ppermute(part, 'tensor', routes[kind])  60.1 us
    pallas_call x4, Pallas kernels, backward_scan(): pl.pallas_call(backward_kernel, grid=(chunks,), in_specs=sequence_specs(s...  57.9 us
    pallas_call x4, Pallas kernels, normed_gradient(): pl.pallas_call(normed_kernel, grid=(width // tile,), in_specs=[whole_spec...  40.4 us
    unnamed x263, local copies, waits for them, and re-layouts  37.4 us
    psum x1, blocking collectives, shards(): total = lax.psum(jnp.concatenate(stats, 0), 'tensor')  33 us
    add x10, other arithmetic, turn(): send.append(('across', name, own + got, None))  24.9 us
  transfers between devices with their start and end apart: 29, of which 12 were waited for; matrix products, arithmetic and copies ran while one was open for 24% of the time, Pallas kernels for 18%

profile of v2, /device:TPU:0, one launch (start us, length us, event | category | flops | bytes accessed | tf_op | source)
XLA Modules:
  0.0 635.2 jit_solution(2732365946095174699)
XLA Ops:
  30.1 4.8 forward_scan.4
  37.6 6.7 %collective-permute-start = (f32[256,2048]{1,0:T(8,128)}, f32[256,2048]{1,0:T(8,128)}, u32[]{:S(2)}, u32[]{:S(2)}) collective-permute-start(f32[256,2048]{1,0:T(8,128)} %fusion.106), channel_id=1, source_target_pairs={{0,1},{3,2},{4,5},{7,6},{8,9},{11,10},{12,13},{15,14},{16,17},{19,... | collective-permute-start | bytes 6291464 | tf_op jit(solution)/shard_map/ppermute | solution.py:619
  60.4 4.8 forward_scan.5
  78.6 4.9 forward_scan.6
  88.7 5.1 fusion.114
  96.4 4.3 add.230
  114.4 5.8 forward_scan.7
  122.3 33.0 %psum.35 = f32[1024,2]{0,1:T(2,128)S(1)} all-reduce(f32[1024,2]{0,1:T(2,128)S(1)} %pad_maximum_fusion.4), channel_id=1, replica_groups=mesh['dp'=8,'tensor'=4] {'tensor'}, use_global_device_ids=true, to_apply=%region_4.5 | all-reduce | flops 2048 | bytes 16384 | tf_op jit(solution)/shard_map/psum | solution.py:737
  172.7 14.5 %backward_scan.4 = (bf16[256,1024]{1,0:T(8,128)(2,1)}, bf16[256,1024]{1,0:T(8,128)(2,1)}, bf16[256,384]{1,0:T(8,128)(2,1)}, f32[128,1024]{1,0:T(8,128)}, f32[8,1...) custom-call(f32[256,1024]{1,0:T(8,128)} %copy-done.7, ...), custom_call_target="tpu_custom_call" | custom-call | tf_op jit(solution)/shard_map/backward_scan/pallas_call | solution.py:419
  187.2 10.0 %normed_gradient.4 = (f32[256,2048]{1,0:T(8,128)}, f32[8,2048]{1,0:T(8,128)}) custom-call(bf16[256,1024]{1,0:T(8,128)(2,1)} %get-tuple-element.267.d_z, bf16[256,1024]{1,0:T(8,128)(2,1)} %get-tuple-element.268.d_x, bf16[256,384]{1,0:T(8,128)(2,1)} %get-tuple-element.269.d_rest, bf16[2048,1024]{1,0:T(8,128)(2,1)} %z_weight.7, bf16[2048,1024]{1,0:T(8,128)(2,1)} %x_weight.7, ...), custom_call_target="tpu_custom_call" | custom-call | tf_op jit(solution)/shard_map/normed_gradient/pallas_call | solution.py:488
  197.3 9.3 %fusion = f32[1024,2048]{1,0:T(8,128)} fusion(bf16[1024,2048]{1,0:T(8,128)(2,1)} %param.32, f32[1024]{0:T(1024)S(1)} %bitcast.101, bf16[256,1024]{1,0:T(8,128)(2,1)S(1)} %get-tuple-element.257, bf16[256,1024]{1,0:T(8,128)(2,1)S(1)} %copy-done.45, bf16[256,1024]{1,0:T(8,128)(2,1)S(1)} %copy-done.43, bf16[256,1024]{1,0:T(8,128)(2,1)S(1)} %copy-done.41), kind=kOutput, calls=%fused_computation.1 | convolution fusion | flops 4309647360 | bytes 14684160 | tf_op jit(solution)/shard_map/dot_general | solution.py:25
  206.5 4.5 collective-permute-done.3
  223.8 14.6 %backward_scan.5 = (bf16[256,1024]{1,0:T(8,128)(2,1)}, bf16[256,1024]{1,0:T(8,128)(2,1)}, bf16[256,384]{1,0:T(8,128)(2,1)}, f32[128,1024]{1,0:T(8,128)}, f32[8,1...) custom-call(f32[256,1024]{1,0:T(8,128)} %copy-done.3, ...), custom_call_target="tpu_custom_call" | custom-call | tf_op jit(solution)/shard_map/backward_scan/pallas_call | solution.py:419
  238.5 10.4 %normed_gradient.5 = (f32[256,2048]{1,0:T(8,128)}, f32[8,2048]{1,0:T(8,128)}) custom-call(bf16[256,1024]{1,0:T(8,128)(2,1)} %get-tuple-element.287.d_z, bf16[256,1024]{1,0:T(8,128)(2,1)} %get-tuple-element.288.d_x, bf16[256,384]{1,0:T(8,128)(2,1)} %get-tuple-element.289.d_rest, bf16[2048,1024]{1,0:T(8,128)(2,1)} %z_weight.7, bf16[2048,1024]{1,0:T(8,128)(2,1)} %x_weight.7, ...), custom_call_target="tpu_custom_call" | custom-call | tf_op jit(solution)/shard_map/normed_gradient/pallas_call | solution.py:488
  249.7 16.5 %collective-permute-done.5 = f32[256,2048]{1,0:T(8,128)S(1)} collective-permute-done((f32[256,2048]{1,0:T(8,128)}, f32[256,2048]{1,0:T(8,128)S(1)}, u32[]{:S(2)}, u32[]{:S(2)}) %collective-permute-start.5) | collective-permute-done | bytes 2097184 | tf_op jit(solution)/shard_map/ppermute | solution.py:619
  276.9 14.3 %backward_scan.6 = (bf16[256,1024]{1,0:T(8,128)(2,1)}, bf16[256,1024]{1,0:T(8,128)(2,1)}, bf16[256,384]{1,0:T(8,128)(2,1)}, f32[128,1024]{1,0:T(8,128)}, f32[8,1...) custom-call(f32[256,1024]{1,0:T(8,128)} %copy-done.2, ...), custom_call_target="tpu_custom_call" | custom-call | tf_op jit(solution)/shard_map/backward_scan/pallas_call | solution.py:419
  291.2 9.9 %normed_gradient.6 = (f32[256,2048]{1,0:T(8,128)}, f32[8,2048]{1,0:T(8,128)}) custom-call(bf16[256,1024]{1,0:T(8,128)(2,1)} %get-tuple-element.327.d_z, bf16[256,1024]{1,0:T(8,128)(2,1)} %get-tuple-element.328.d_x, bf16[256,384]{1,0:T(8,128)(2,1)} %get-tuple-element.329.d_rest, bf16[2048,1024]{1,0:T(8,128)(2,1)} %z_weight.7, bf16[2048,1024]{1,0:T(8,128)(2,1)} %x_weight.7, ...), custom_call_target="tpu_custom_call" | custom-call | tf_op jit(solution)/shard_map/normed_gradient/pallas_call | solution.py:488
  302.0 16.2 %collective-permute-done.7 = f32[256,2048]{1,0:T(8,128)S(1)} collective-permute-done((f32[256,2048]{1,0:T(8,128)S(1)}, f32[256,2048]{1,0:T(8,128)S(1)}, u32[]{:S(2)}, u32[]{:S(2)}) %collective-permute-start.7) | collective-permute-done | bytes 2097184 | tf_op jit(solution)/shard_map/ppermute | solution.py:619
  330.3 14.4 %backward_scan.7 = (bf16[256,1024]{1,0:T(8,128)(2,1)}, bf16[256,1024]{1,0:T(8,128)(2,1)}, bf16[256,384]{1,0:T(8,128)(2,1)}, f32[128,1024]{1,0:T(8,128)}, f32[8,1...) custom-call(f32[256,1024]{1,0:T(8,128)} %copy-done, ...), custom_call_target="tpu_custom_call" | custom-call | tf_op jit(solution)/shard_map/backward_scan/pallas_call | solution.py:419
  349.4 6.1 fusion.96
  355.6 10.1 %normed_gradient.7 = (f32[256,2048]{1,0:T(8,128)}, f32[8,2048]{1,0:T(8,128)}) custom-call(bf16[256,1024]{1,0:T(8,128)(2,1)} %get-tuple-element.346.d_z, bf16[256,1024]{1,0:T(8,128)(2,1)} %get-tuple-element.347.d_x, bf16[256,384]{1,0:T(8,128)(2,1)} %get-tuple-element.348.d_rest, bf16[2048,1024]{1,0:T(8,128)(2,1)} %z_weight.7, bf16[2048,1024]{1,0:T(8,128)(2,1)} %x_weight.7, ...), custom_call_target="tpu_custom_call" | custom-call | tf_op jit(solution)/shard_map/normed_gradient/pallas_call | solution.py:488
  373.5 4.3 add_select_fusion
  386.1 6.9 %fusion.97 = f32[2048,1024]{1,0:T(8,128)} fusion(bf16[1024,1024]{1,0:T(8,128)(2,1)S(1)} %copy-done.91, bf16[256,2048]{1,0:T(8,128)(2,1)S(1)} %copy-done.85, bf16[256,2048]{1,0:T(8,128)(2,1)S(1)} %copy-done.87, bf16[256,2048]{1,0:T(8,128)(2,1)S(1)} %copy-done.89, bf16[256,2048]{1,0:T(8,128)(2,1)S(1)} %copy-done.83), kind=kOutput, calls=%fused_computation.183 | convolution fusion | flops 4311744512 | bytes 14680064 | tf_op jit(solution)/shard_map/dot_general | solution.py:25
  393.0 26.4 %collective-permute-done.11 = f32[256,2048]{1,0:T(8,128)S(1)} collective-permute-done((f32[256,2048]{1,0:T(8,128)}, f32[256,2048]{1,0:T(8,128)S(1)}, u32[]{:S(2)}, u32[]{:S(2)}) %collective-permute-start.11) | collective-permute-done | bytes 2097184 | tf_op jit(solution)/shard_map/ppermute | solution.py:619
  429.8 9.8 %collective-permute-start.13 = (f32[128,2048]{1,0:T(8,128)}, f32[128,2048]{1,0:T(8,128)}, u32[]{:S(2)}, u32[]{:S(2)}) collective-permute-start(f32[128,2048]{1,0:T(8,128)} %get-tuple-element.380), channel_id=1, source_target_pairs={{0,1},{3,2},{4,5},{7,6},{8,9},{11,10},{12,13},{15,14},{16,17},{19,... | collective-permute-start | bytes 3145736 | tf_op jit(solution)/shard_map/ppermute | solution.py:619
  439.7 23.2 %all-reduce.5 = (f32[2048]{0:T(1024)S(1)}, f32[2048]{0:T(1024)S(1)}, f32[8,1024]{1,0:T(8,128)S(1)}, f32[8,16]{1,0:T(8,128)}) all-reduce(f32[2048]{0:T(1024)S(1)} %bitcast.102, f32[2048]{0:T(1024)S(1)} %bitcast.103, f32[8,1024]{1,0:T(8,128)S(1)} %copy-done.112, f32[8,16]{1,0:T(8,128)S(1)} %copy-done.121), channel_id=1, replica_groups=mesh['dp'=8,'tensor'=4] {'dp'}, use_global_device_ids=true, to_apply=%region_7.8 | all-reduce | flops 12416 | bytes 99328 | tf_op jit(solution)/shard_map/psum | solution.py:775
  462.8 10.7 %fusion.95 = f32[2048,1024]{1,0:T(8,128)} fusion(bf16[1024,1024]{1,0:T(8,128)(2,1)} %pad_maximum_fusion.2, bf16[256,2048]{1,0:T(8,128)(2,1)} %copy-done.84, bf16[256,2048]{1,0:T(8,128)(2,1)} %get-tuple-element.527, bf16[256,2048]{1,0:T(8,128)(2,1)} %copy-done.88, bf16[256,2048]{1,0:T(8,128)(2,1)S(1)} %copy-done.83), kind=kOutput, calls=%fused_computation.181 | convolution fusion | flops 4311744512 | bytes 14680064 | tf_op jit(solution)/shard_map/dot_general | solution.py:25
  479.6 21.1 %reduce-scatter.9.cloned.1.call-done = f32[256,1024]{1,0:T(8,128)} async-done(((f32[2048,1024]{1,0:T(8,128)}), f32[256,1024]{1,0:T(8,128)}) %reduce-scatter.9.cloned.1.call-update) | async-done | bytes 1048592 | tf_op jit(solution)/shard_map/reduce_scatter | solution.py:774
  522.2 8.3 %collective-permute-done.16 = f32[128,2048]{1,0:T(8,128)S(1)} collective-permute-done((f32[128,2048]{1,0:T(8,128)}, f32[128,2048]{1,0:T(8,128)S(1)}, u32[]{:S(2)}, u32[]{:S(2)}) %collective-permute-start.16) | collective-permute-done | bytes 1048608 | tf_op jit(solution)/shard_map/ppermute | solution.py:619
  530.5 27.3 %collective-permute-done.18 = f32[256,2048]{1,0:T(8,128)S(1)} collective-permute-done((f32[256,2048]{1,0:T(8,128)}, f32[256,2048]{1,0:T(8,128)S(1)}, u32[]{:S(2)}, u32[]{:S(2)}) %collective-permute-start.18) | collective-permute-done | bytes 2097184 | tf_op jit(solution)/shard_map/ppermute | solution.py:619
  578.4 10.3 %collective-permute-done.21 = f32[128,2048]{1,0:T(8,128)} collective-permute-done((f32[128,2048]{1,0:T(8,128)S(1)}, f32[128,2048]{1,0:T(8,128)}, u32[]{:S(2)}, u32[]{:S(2)}) %collective-permute-start.21) | collective-permute-done | bytes 1048608 | tf_op jit(solution)/shard_map/ppermute | solution.py:619
  604.6 12.0 %collective-permute-done.23 = f32[128,2048]{1,0:T(8,128)S(1)} collective-permute-done((f32[128,2048]{1,0:T(8,128)S(1)}, f32[128,2048]{1,0:T(8,128)S(1)}, u32[]{:S(2)}, u32[]{:S(2)}) %collective-permute-start.23) | collective-permute-done | bytes 1048608 | tf_op jit(solution)/shard_map/ppermute | solution.py:619
  (441 shorter events, 239.0 us)
Async XLA Ops:
  7.2 342.2 %reduce-scatter.5.cloned.1.call-start = ((), (), s32[]{:S(2)}) async-start(), calls=%async_computation.4 | async-start | bytes 9437184 | tf_op jit(solution)/shard_map/reduce_scatter | solution.py:764
  7.9 106.4 %copy-start.35 = (f32[1024]{0:T(1024)}, f32[1024]{0:T(1024)S(1)}, u32[]{:S(2)}) copy-start(f32[1024]{0:T(1024)S(1)} %convert_element_type.120) | copy-start | bytes 12292
  13.8 100.5 %copy-start.21 = (bf16[16,1024]{1,0:T(8,128)(2,1)}, bf16[16,1024]{1,0:T(8,128)(2,1)S(1)}, u32[]{:S(2)}) copy-start(bf16[16,1024]{1,0:T(8,128)(2,1)S(1)} %fusion.53.spread_ref) | copy-start | bytes 98308
  14.5 99.8 %copy-start.1 = (f32[1024,16]{1,0:T(8,128)}, f32[1024,16]{1,0:T(8,128)S(1)}, u32[]{:S(2)}) copy-start(f32[1024,16]{1,0:T(8,128)S(1)} %copy.109.aux_ref) | copy-start | bytes 196612
  37.6 58.7 %collective-permute-start = (f32[256,2048]{1,0:T(8,128)}, f32[256,2048]{1,0:T(8,128)}, u32[]{:S(2)}, u32[]{:S(2)}) collective-permute-start(f32[256,2048]{1,0:T(8,128)} %fusion.106), channel_id=1, source_target_pairs={{0,1},{3,2},{4,5},{7,6},{8,9},{11,10},{12,13},{15,14},{16,17},{19,... | collective-permute-start | bytes 6291464 | tf_op jit(solution)/shard_map/ppermute | solution.py:619
  100.6 54.7 %collective-permute-start.2 = (f32[256,2048]{1,0:T(8,128)}, f32[256,2048]{1,0:T(8,128)}, u32[]{:S(2)}, u32[]{:S(2)}) collective-permute-start(f32[256,2048]{1,0:T(8,128)} %add.230), channel_id=1, source_target_pairs={{1,2},{2,1},{5,6},{6,5},{9,10},{10,9},{13,14},{14,13},{17,18},{18,... | collective-permute-start | bytes 6291464 | tf_op jit(solution)/shard_map/ppermute | solution.py:619
  102.6 52.7 %collective-permute-start.1 = (f32[256,2048]{1,0:T(8,128)}, f32[256,2048]{1,0:T(8,128)}, u32[]{:S(2)}, u32[]{:S(2)}) collective-permute-start(f32[256,2048]{1,0:T(8,128)} %fusion.114), channel_id=1, source_target_pairs={{0,1},{3,2},{4,5},{7,6},{8,9},{11,10},{12,13},{15,14},{16,17},{19,... | collective-permute-start | bytes 6291464 | tf_op jit(solution)/shard_map/ppermute | solution.py:619
  163.5 43.0 %collective-permute-start.4 = (f32[256,2048]{1,0:T(8,128)}, f32[256,2048]{1,0:T(8,128)}, u32[]{:S(2)}, u32[]{:S(2)}) collective-permute-start(f32[256,2048]{1,0:T(8,128)} %add.233), channel_id=1, source_target_pairs={{1,2},{2,1},{5,6},{6,5},{9,10},{10,9},{13,14},{14,13},{17,18},{18,... | collective-permute-start | bytes 6291464 | tf_op jit(solution)/shard_map/ppermute | solution.py:619
  165.7 45.3 %collective-permute-start.3 = (f32[256,2048]{1,0:T(8,128)}, f32[256,2048]{1,0:T(8,128)S(1)}, u32[]{:S(2)}, u32[]{:S(2)}) collective-permute-start(f32[256,2048]{1,0:T(8,128)} %add_select_fusion.4), channel_id=1, source_target_pairs={{0,1},{3,2},{1,0},{2,3},{4,5},{7,6},{5,4},{6,7},{8,9},{11,10},{9,8... | collective-permute-start | bytes 6291464 | tf_op jit(solution)/shard_map/ppermute | solution.py:619
  219.1 200.3 %reduce-scatter.7.cloned.1.call-start = ((), (), s32[]{:S(2)}) async-start(), calls=%async_computation.5 | async-start | bytes 3538944 | tf_op jit(solution)/shard_map/reduce_scatter | solution.py:772
  219.1 30.6 %collective-permute-start.6 = (f32[256,2048]{1,0:T(8,128)}, f32[256,2048]{1,0:T(8,128)S(1)}, u32[]{:S(2)}, u32[]{:S(2)}) collective-permute-start(f32[256,2048]{1,0:T(8,128)} %add.237), channel_id=1, source_target_pairs={{1,2},{2,1},{5,6},{6,5},{9,10},{10,9},{13,14},{14,13},{17,18},{18,... | collective-permute-start | bytes 6291464 | tf_op jit(solution)/shard_map/ppermute | solution.py:619
  220.2 46.0 %collective-permute-start.5 = (f32[256,2048]{1,0:T(8,128)}, f32[256,2048]{1,0:T(8,128)S(1)}, u32[]{:S(2)}, u32[]{:S(2)}) collective-permute-start(f32[256,2048]{1,0:T(8,128)} %add_select_fusion.3), channel_id=1, source_target_pairs={{0,1},{3,2},{1,0},{2,3},{4,5},{7,6},{5,4},{6,7},{8,9},{11,10},{9,8... | collective-permute-start | bytes 6291464 | tf_op jit(solution)/shard_map/ppermute | solution.py:619
  272.1 29.9 %collective-permute-start.8 = (f32[256,2048]{1,0:T(8,128)}, f32[256,2048]{1,0:T(8,128)}, u32[]{:S(2)}, u32[]{:S(2)}) collective-permute-start(f32[256,2048]{1,0:T(8,128)} %add.240), channel_id=1, source_target_pairs={{1,2},{2,1},{5,6},{6,5},{9,10},{10,9},{13,14},{14,13},{17,18},{18,... | collective-permute-start | bytes 6291464 | tf_op jit(solution)/shard_map/ppermute | solution.py:619
  274.5 43.7 %collective-permute-start.7 = (f32[256,2048]{1,0:T(8,128)S(1)}, f32[256,2048]{1,0:T(8,128)S(1)}, u32[]{:S(2)}, u32[]{:S(2)}) collective-permute-start(f32[256,2048]{1,0:T(8,128)S(1)} %add_select_fusion.2), channel_id=1, source_target_pairs={{0,1},{3,2},{1,0},{2,3},{4,5},{7,6},{5,4},{6,7},{8,9},{11,10},{9,8... | collective-permute-start | bytes 6291464 | tf_op jit(solution)/shard_map/ppermute | solution.py:619
  325.3 41.2 %collective-permute-start.10 = (f32[256,2048]{1,0:T(8,128)}, f32[256,2048]{1,0:T(8,128)}, u32[]{:S(2)}, u32[]{:S(2)}) collective-permute-start(f32[256,2048]{1,0:T(8,128)} %add.243), channel_id=1, source_target_pairs={{1,2},{2,1},{5,6},{6,5},{9,10},{10,9},{13,14},{14,13},{17,18},{18,... | collective-permute-start | bytes 6291464 | tf_op jit(solution)/shard_map/ppermute | solution.py:619
  327.5 42.9 %collective-permute-start.9 = (f32[256,2048]{1,0:T(8,128)}, f32[256,2048]{1,0:T(8,128)S(1)}, u32[]{:S(2)}, u32[]{:S(2)}) collective-permute-start(f32[256,2048]{1,0:T(8,128)} %add_select_fusion.1), channel_id=1, source_target_pairs={{0,1},{3,2},{1,0},{2,3},{4,5},{7,6},{5,4},{6,7},{8,9},{11,10},{9,8... | collective-permute-start | bytes 6291464 | tf_op jit(solution)/shard_map/ppermute | solution.py:619
  355.6 145.1 %reduce-scatter.9.cloned.1.call-start = ((), (), s32[]{:S(2)}) async-start(), calls=%async_computation.6 | async-start | bytes 9437184 | tf_op jit(solution)/shard_map/reduce_scatter | solution.py:774
  377.8 41.5 %collective-permute-start.11 = (f32[256,2048]{1,0:T(8,128)}, f32[256,2048]{1,0:T(8,128)S(1)}, u32[]{:S(2)}, u32[]{:S(2)}) collective-permute-start(f32[256,2048]{1,0:T(8,128)} %add_select_fusion), channel_id=1, source_target_pairs={{0,1},{3,2},{1,0},{2,3},{4,5},{7,6},{5,4},{6,7},{8,9},{11,10},{9,8... | collective-permute-start | bytes 6291464 | tf_op jit(solution)/shard_map/ppermute | solution.py:619
  379.6 39.8 %collective-permute-start.12 = (f32[256,2048]{1,0:T(8,128)}, f32[256,2048]{1,0:T(8,128)}, u32[]{:S(2)}, u32[]{:S(2)}) collective-permute-start(f32[256,2048]{1,0:T(8,128)} %add.246), channel_id=1, source_target_pairs={{1,2},{2,1},{5,6},{6,5},{9,10},{10,9},{13,14},{14,13},{17,18},{18,... | collective-permute-start | bytes 6291464 | tf_op jit(solution)/shard_map/ppermute | solution.py:619
  426.4 201.8 %reduce-scatter.11.cloned.1.call-start = ((), (), s32[]{:S(2)}) async-start(), calls=%async_computation.7 | async-start | bytes 9437184 | tf_op jit(solution)/shard_map/reduce_scatter | solution.py:779
  426.5 47.1 %collective-permute-start.14 = (f32[256,2048]{1,0:T(8,128)}, f32[256,2048]{1,0:T(8,128)}, u32[]{:S(2)}, u32[]{:S(2)}) collective-permute-start(f32[256,2048]{1,0:T(8,128)} %add.247), channel_id=1, source_target_pairs={{1,2},{2,1},{5,6},{6,5},{9,10},{10,9},{13,14},{14,13},{17,18},{18,... | collective-permute-start | bytes 6291464 | tf_op jit(solution)/shard_map/ppermute | solution.py:619
  428.5 45.7 %collective-permute-start.15 = (f32[256,2048]{1,0:T(8,128)}, f32[256,2048]{1,0:T(8,128)}, u32[]{:S(2)}, u32[]{:S(2)}) collective-permute-start(f32[256,2048]{1,0:T(8,128)} %add.248), channel_id=1, source_target_pairs={{1,0},{2,3},{5,4},{6,7},{9,8},{10,11},{13,12},{14,15},{17,16},{18,... | collective-permute-start | bytes 6291464 | tf_op jit(solution)/shard_map/ppermute | solution.py:619
  429.8 43.8 %collective-permute-start.13 = (f32[128,2048]{1,0:T(8,128)}, f32[128,2048]{1,0:T(8,128)}, u32[]{:S(2)}, u32[]{:S(2)}) collective-permute-start(f32[128,2048]{1,0:T(8,128)} %get-tuple-element.380), channel_id=1, source_target_pairs={{0,1},{3,2},{4,5},{7,6},{8,9},{11,10},{12,13},{15,14},{16,17},{19,... | collective-permute-start | bytes 3145736 | tf_op jit(solution)/shard_map/ppermute | solution.py:619
  504.4 26.1 %collective-permute-start.16 = (f32[128,2048]{1,0:T(8,128)}, f32[128,2048]{1,0:T(8,128)S(1)}, u32[]{:S(2)}, u32[]{:S(2)}) collective-permute-start(f32[128,2048]{1,0:T(8,128)} %get-tuple-element.389), channel_id=1, source_target_pairs={{0,1},{3,2},{4,5},{7,6},{8,9},{11,10},{12,13},{15,14},{16,17},{19,... | collective-permute-start | bytes 3145736 | tf_op jit(solution)/shard_map/ppermute | solution.py:619
  507.9 22.6 %collective-permute-start.17 = (f32[128,2048]{1,0:T(8,128)S(1)}, f32[128,2048]{1,0:T(8,128)S(1)}, u32[]{:S(2)}, u32[]{:S(2)}) collective-permute-start(f32[128,2048]{1,0:T(8,128)S(1)} %add.249), channel_id=1, source_target_pairs={{1,2},{2,1},{5,6},{6,5},{9,10},{10,9},{13,14},{14,13},{17,18},{18,... | collective-permute-start | bytes 3145736 | tf_op jit(solution)/shard_map/ppermute | solution.py:619
  508.6 49.2 %collective-permute-start.18 = (f32[256,2048]{1,0:T(8,128)}, f32[256,2048]{1,0:T(8,128)S(1)}, u32[]{:S(2)}, u32[]{:S(2)}) collective-permute-start(f32[256,2048]{1,0:T(8,128)} %add.250), channel_id=1, source_target_pairs={{1,0},{2,3},{5,4},{6,7},{9,8},{10,11},{13,12},{14,15},{17,16},{18,... | collective-permute-start | bytes 6291464 | tf_op jit(solution)/shard_map/ppermute | solution.py:619
  559.2 19.2 %collective-permute-start.19 = (f32[40,2048]{1,0:T(8,128)S(1)}, f32[40,2048]{1,0:T(8,128)}, u32[]{:S(2)}, u32[]{:S(2)}) collective-permute-start(f32[40,2048]{1,0:T(8,128)S(1)} %copy-done.102), channel_id=1, source_target_pairs={{0,1},{3,2},{4,5},{7,6},{8,9},{11,10},{12,13},{15,14},{16,17},{19,... | collective-permute-start | bytes 983048 | tf_op jit(solution)/shard_map/ppermute | solution.py:619
  561.6 16.8 %collective-permute-start.20 = (f32[128,2048]{1,0:T(8,128)}, f32[128,2048]{1,0:T(8,128)}, u32[]{:S(2)}, u32[]{:S(2)}) collective-permute-start(f32[128,2048]{1,0:T(8,128)} %add.255), channel_id=1, source_target_pairs={{1,2},{2,1},{5,6},{6,5},{9,10},{10,9},{13,14},{14,13},{17,18},{18,... | collective-permute-start | bytes 3145736 | tf_op jit(solution)/shard_map/ppermute | solution.py:619
  563.2 25.4 %collective-permute-start.21 = (f32[128,2048]{1,0:T(8,128)S(1)}, f32[128,2048]{1,0:T(8,128)}, u32[]{:S(2)}, u32[]{:S(2)}) collective-permute-start(f32[128,2048]{1,0:T(8,128)S(1)} %add.256), channel_id=1, source_target_pairs={{1,0},{2,3},{5,4},{6,7},{9,8},{10,11},{13,12},{14,15},{17,16},{18,... | collective-permute-start | bytes 3145736 | tf_op jit(solution)/shard_map/ppermute | solution.py:619
  592.2 24.4 %collective-permute-start.23 = (f32[128,2048]{1,0:T(8,128)S(1)}, f32[128,2048]{1,0:T(8,128)S(1)}, u32[]{:S(2)}, u32[]{:S(2)}) collective-permute-start(f32[128,2048]{1,0:T(8,128)S(1)} %add.261), channel_id=1, source_target_pairs={{1,0},{2,3},{5,4},{6,7},{9,8},{10,11},{13,12},{14,15},{17,16},{18,... | collective-permute-start | bytes 3145736 | tf_op jit(solution)/shard_map/ppermute | solution.py:619
  599.2 5.4 collective-permute-start.22
  616.6 9.0 %collective-permute-start.24 = (f32[40,2048]{1,0:T(8,128)S(1)}, f32[40,2048]{1,0:T(8,128)S(1)}, u32[]{:S(2)}, u32[]{:S(2)}) collective-permute-start(f32[40,2048]{1,0:T(8,128)S(1)} %add.263), channel_id=1, source_target_pairs={{1,0},{2,3},{5,4},{6,7},{9,8},{10,11},{13,12},{14,15},{17,16},{18,... | collective-permute-start | bytes 983048 | tf_op jit(solution)/shard_map/ppermute | solution.py:619
  (126 other events, 1186.4 us)
Sparse Core Ops, SparseCore 0:
  219.2 70.8 reduce-scatter.4
  355.7 45.7 reduce-scatter.6
  426.5 74.0 reduce-scatter.8
  505.0 71.2 reduce-scatter.10

commit v3 on v2

--- a/solution.py
+++ b/solution.py
@@ -773,19 +773,15 @@
     z_grad, d_x, rest_share, *carried = line.turn((z_grad, d_x, rest_share, *carried))
     z_share = lax.psum_scatter(z_grad, "dp", scatter_dimension=0, tiled=True)
     norm_grad, g_chan, g_bc, g_head = lax.psum((norm_grad[0], *carried[3:]), "dp")
-    x_grad = contract_rows(normed_all, d_x)
-    x_grad, norm_grad = line.turn((x_grad, norm_grad))
-    x_grad, z_share = lax.optimization_barrier((x_grad, z_share))
-    x_share = lax.psum_scatter(x_grad, "dp", scatter_dimension=0, tiled=True)
-
     bc_part = rest_share[:, : 2 * STATE]
     extra = jnp.concatenate([norm_grad, g_bc.reshape(-1), bc_part.reshape(-1)])
     extra_rows = -(-extra.shape[0] // (8 * width)) * 8
     extra = jnp.pad(extra, (0, extra_rows * width - extra.shape[0])).reshape(extra_rows, width)
-    extra = line.start_finishing(
-        Finish(hidden_in, cotangent, norm_gain, rms_all, scale), extra
-    )
     line.add(("extra", 0, extra_rows), extra)
+    (d_x,) = line.turn((d_x,))
+    d_x = line.start_finishing(Finish(hidden_in, cotangent, norm_gain, rms_all, scale), d_x)
+    x_grad = contract_rows(normed_all, d_x)
+    x_share = lax.psum_scatter(x_grad, "dp", scatter_dimension=0, tiled=True)
 
     while line.busy():
         line.turn()

time: 645 us -> 610 us (0.946)
  waiting for transfers between devices: 151 us -> 123 us
    reduce_scatter x1, waiting for transfers between devices: 21.1 us -> 0.01 us  [shards(): z_share = lax.psum_scatter(z_grad, 'dp', scatter_dimension=0, tiled=True)]
    ppermute x25, waiting for transfers between devices: 130 us -> 123 us  [turn(): moved = lax.ppermute(part, 'tensor', routes[kind])]
    unnamed x263 -> x269, local copies, waits for them, and re-layouts: 37.4 us -> 37.3 us
  transfers between devices with their start and end apart: 29 -> 29, of which waited for: 12 -> 10; matrix products, arithmetic and copies ran while one was open for 24% -> 25% of each run, Pallas kernels for 18% -> 19%
where the time goes in v3:
time: 610 us; the launch traced here: 600 us
  waiting for transfers between devices  123 us (20%)
  Pallas kernels  119 us (20%)
  other arithmetic  98.4 us (16%)
  matrix products  72.7 us (12%)
  local copies, waits for them, and re-layouts  57.6 us (9%)
  starting transfers between devices  57.4 us (9%)
  blocking collectives  56.8 us (9%)
  between operations  15.8 us (3%)
    ppermute x25, waiting for transfers between devices, turn(): moved = lax.ppermute(part, 'tensor', routes[kind])  123 us
    dot_general x24, matrix products, dot(): lax.dot_general(left, right, (dims, ((), ())), preferred_element_type=f32)  72.7 us
    pallas_call x4, Pallas kernels, backward_scan(): pl.pallas_call(backward_kernel, grid=(chunks,), in_specs=sequence_specs(s...  57.8 us
    ppermute x25, starting transfers between devices, turn(): moved = lax.ppermute(part, 'tensor', routes[kind])  57.2 us
    pallas_call x4, Pallas kernels, normed_gradient(): pl.pallas_call(normed_kernel, grid=(width // tile,), in_specs=[whole_spec...  40.5 us
    unnamed x269, local copies, waits for them, and re-layouts  37.3 us
    psum x1, blocking collectives, shards(): total = lax.psum(jnp.concatenate(stats, 0), 'tensor')  33 us
    add x10, other arithmetic, turn(): send.append(('across', name, own + got, None))  24 us
  transfers between devices with their start and end apart: 29, of which 10 were waited for; matrix products, arithmetic and copies ran while one was open for 25% of the time, Pallas kernels for 19%

profile of v3, /device:TPU:0, one launch (start us, length us, event | category | flops | bytes accessed | tf_op | source)
XLA Modules:
  0.0 600.0 jit_solution(17470825573380393083)
XLA Ops:
  30.1 4.8 forward_scan.4
  37.6 6.7 %collective-permute-start = (f32[256,2048]{1,0:T(8,128)}, f32[256,2048]{1,0:T(8,128)}, u32[]{:S(2)}, u32[]{:S(2)}) collective-permute-start(f32[256,2048]{1,0:T(8,128)} %fusion.106), channel_id=1, source_target_pairs={{0,1},{3,2},{4,5},{7,6},{8,9},{11,10},{12,13},{15,14},{16,17},{19,... | collective-permute-start | bytes 6291464 | tf_op jit(solution)/shard_map/ppermute | solution.py:619
  60.4 4.8 forward_scan.5
  78.6 4.9 forward_scan.6
  88.8 5.1 fusion.114
  96.4 4.3 add.230
  114.5 5.7 forward_scan.7
  122.3 33.0 %psum.35 = f32[1024,2]{0,1:T(2,128)S(1)} all-reduce(f32[1024,2]{0,1:T(2,128)S(1)} %pad_maximum_fusion.4), channel_id=1, replica_groups=mesh['dp'=8,'tensor'=4] {'tensor'}, use_global_device_ids=true, to_apply=%region_4.5 | all-reduce | flops 2048 | bytes 16384 | tf_op jit(solution)/shard_map/psum | solution.py:737
  159.3 4.2 add_select_fusion.4
  172.7 14.4 %backward_scan.4 = (bf16[256,1024]{1,0:T(8,128)(2,1)}, bf16[256,1024]{1,0:T(8,128)(2,1)}, bf16[256,384]{1,0:T(8,128)(2,1)}, f32[128,1024]{1,0:T(8,128)}, f32[8,1...) custom-call(f32[256,1024]{1,0:T(8,128)} %copy-done.7, ...), custom_call_target="tpu_custom_call" | custom-call | tf_op jit(solution)/shard_map/backward_scan/pallas_call | solution.py:419
  187.1 10.0 %normed_gradient.4 = (f32[256,2048]{1,0:T(8,128)}, f32[8,2048]{1,0:T(8,128)}) custom-call(bf16[256,1024]{1,0:T(8,128)(2,1)} %get-tuple-element.263.d_z, bf16[256,1024]{1,0:T(8,128)(2,1)} %get-tuple-element.264.d_x, bf16[256,384]{1,0:T(8,128)(2,1)} %get-tuple-element.265.d_rest, bf16[2048,1024]{1,0:T(8,128)(2,1)} %z_weight.7, bf16[2048,1024]{1,0:T(8,128)(2,1)} %x_weight.7, ...), custom_call_target="tpu_custom_call" | custom-call | tf_op jit(solution)/shard_map/normed_gradient/pallas_call | solution.py:488
  197.2 9.3 %fusion = f32[1024,2048]{1,0:T(8,128)} fusion(bf16[1024,2048]{1,0:T(8,128)(2,1)} %param.32, f32[1024]{0:T(1024)S(1)} %bitcast.101, bf16[256,1024]{1,0:T(8,128)(2,1)S(1)} %get-tuple-element.253, bf16[256,1024]{1,0:T(8,128)(2,1)S(1)} %copy-done.45, bf16[256,1024]{1,0:T(8,128)(2,1)S(1)} %copy-done.43, bf16[256,1024]{1,0:T(8,128)(2,1)S(1)} %copy-done.41), kind=kOutput, calls=%fused_computation.1 | convolution fusion | flops 4309647360 | bytes 14684160 | tf_op jit(solution)/shard_map/dot_general | solution.py:25
  206.4 4.6 collective-permute-done.3
  223.9 14.6 %backward_scan.5 = (bf16[256,1024]{1,0:T(8,128)(2,1)}, bf16[256,1024]{1,0:T(8,128)(2,1)}, bf16[256,384]{1,0:T(8,128)(2,1)}, f32[128,1024]{1,0:T(8,128)}, f32[8,1...) custom-call(f32[256,1024]{1,0:T(8,128)} %copy-done.3, ...), custom_call_target="tpu_custom_call" | custom-call | tf_op jit(solution)/shard_map/backward_scan/pallas_call | solution.py:419
  238.5 10.4 %normed_gradient.5 = (f32[256,2048]{1,0:T(8,128)}, f32[8,2048]{1,0:T(8,128)}) custom-call(bf16[256,1024]{1,0:T(8,128)(2,1)} %get-tuple-element.283.d_z, bf16[256,1024]{1,0:T(8,128)(2,1)} %get-tuple-element.284.d_x, bf16[256,384]{1,0:T(8,128)(2,1)} %get-tuple-element.285.d_rest, bf16[2048,1024]{1,0:T(8,128)(2,1)} %z_weight.7, bf16[2048,1024]{1,0:T(8,128)(2,1)} %x_weight.7, ...), custom_call_target="tpu_custom_call" | custom-call | tf_op jit(solution)/shard_map/normed_gradient/pallas_call | solution.py:488
  249.8 16.5 %collective-permute-done.5 = f32[256,2048]{1,0:T(8,128)S(1)} collective-permute-done((f32[256,2048]{1,0:T(8,128)}, f32[256,2048]{1,0:T(8,128)S(1)}, u32[]{:S(2)}, u32[]{:S(2)}) %collective-permute-start.5) | collective-permute-done | bytes 2097184 | tf_op jit(solution)/shard_map/ppermute | solution.py:619
  276.9 14.3 %backward_scan.6 = (bf16[256,1024]{1,0:T(8,128)(2,1)}, bf16[256,1024]{1,0:T(8,128)(2,1)}, bf16[256,384]{1,0:T(8,128)(2,1)}, f32[128,1024]{1,0:T(8,128)}, f32[8,1...) custom-call(f32[256,1024]{1,0:T(8,128)} %copy-done.2, ...), custom_call_target="tpu_custom_call" | custom-call | tf_op jit(solution)/shard_map/backward_scan/pallas_call | solution.py:419
  291.2 9.9 %normed_gradient.6 = (f32[256,2048]{1,0:T(8,128)}, f32[8,2048]{1,0:T(8,128)}) custom-call(bf16[256,1024]{1,0:T(8,128)(2,1)} %get-tuple-element.323.d_z, bf16[256,1024]{1,0:T(8,128)(2,1)} %get-tuple-element.324.d_x, bf16[256,384]{1,0:T(8,128)(2,1)} %get-tuple-element.325.d_rest, bf16[2048,1024]{1,0:T(8,128)(2,1)} %z_weight.7, bf16[2048,1024]{1,0:T(8,128)(2,1)} %x_weight.7, ...), custom_call_target="tpu_custom_call" | custom-call | tf_op jit(solution)/shard_map/normed_gradient/pallas_call | solution.py:488
  302.0 16.3 %collective-permute-done.7 = f32[256,2048]{1,0:T(8,128)S(1)} collective-permute-done((f32[256,2048]{1,0:T(8,128)S(1)}, f32[256,2048]{1,0:T(8,128)S(1)}, u32[]{:S(2)}, u32[]{:S(2)}) %collective-permute-start.7) | collective-permute-done | bytes 2097184 | tf_op jit(solution)/shard_map/ppermute | solution.py:619
  330.4 14.4 %backward_scan.7 = (bf16[256,1024]{1,0:T(8,128)(2,1)}, bf16[256,1024]{1,0:T(8,128)(2,1)}, bf16[256,384]{1,0:T(8,128)(2,1)}, f32[128,1024]{1,0:T(8,128)}, f32[8,1...) custom-call(f32[256,1024]{1,0:T(8,128)} %copy-done, ...), custom_call_target="tpu_custom_call" | custom-call | tf_op jit(solution)/shard_map/backward_scan/pallas_call | solution.py:419
  349.5 6.1 %fusion.96 = f32[2048,384]{1,0:T(8,128)} fusion(bf16[1024,384]{1,0:T(8,128)(2,1)} %pad_maximum_fusion.3, bf16[256,2048]{1,0:T(8,128)(2,1)} %copy-done.85, bf16[256,2048]{1,0:T(8,128)(2,1)} %get-tuple-element.519, bf16[256,2048]{1,0:T(8,128)(2,1)} %copy-done.91, bf16[256,2048]{1,0:T(8,128)(2,1)S(1)} %copy-done.83), kind=kOutput, calls=%fused_computation.182 | convolution fusion | flops 1627389952 | bytes 8126464 | tf_op jit(solution)/shard_map/dot_general | solution.py:25
  355.7 10.2 %normed_gradient.7 = (f32[256,2048]{1,0:T(8,128)}, f32[8,2048]{1,0:T(8,128)}) custom-call(bf16[256,1024]{1,0:T(8,128)(2,1)} %get-tuple-element.342.d_z, bf16[256,1024]{1,0:T(8,128)(2,1)} %get-tuple-element.343.d_x, bf16[256,384]{1,0:T(8,128)(2,1)} %get-tuple-element.344.d_rest, bf16[2048,1024]{1,0:T(8,128)(2,1)} %z_weight.7, bf16[2048,1024]{1,0:T(8,128)(2,1)} %x_weight.7, ...), custom_call_target="tpu_custom_call" | custom-call | tf_op jit(solution)/shard_map/normed_gradient/pallas_call | solution.py:488
  373.6 4.4 add_select_fusion
  386.2 6.9 %fusion.97 = f32[2048,1024]{1,0:T(8,128)} fusion(bf16[1024,1024]{1,0:T(8,128)(2,1)S(1)} %copy-done.97, bf16[256,2048]{1,0:T(8,128)(2,1)S(1)} %copy-done.86, bf16[256,2048]{1,0:T(8,128)(2,1)S(1)} %copy-done.89, bf16[256,2048]{1,0:T(8,128)(2,1)S(1)} %copy-done.92, bf16[256,2048]{1,0:T(8,128)(2,1)S(1)} %copy-done.83), kind=kOutput, calls=%fused_computation.183 | convolution fusion | flops 4311744512 | bytes 14680064 | tf_op jit(solution)/shard_map/dot_general | solution.py:25
  393.1 26.4 %collective-permute-done.11 = f32[256,2048]{1,0:T(8,128)S(1)} collective-permute-done((f32[256,2048]{1,0:T(8,128)}, f32[256,2048]{1,0:T(8,128)S(1)}, u32[]{:S(2)}, u32[]{:S(2)}) %collective-permute-start.11) | collective-permute-done | bytes 2097184 | tf_op jit(solution)/shard_map/ppermute | solution.py:619
  431.8 9.9 %collective-permute-start.13 = (f32[128,2048]{1,0:T(8,128)S(1)}, f32[128,2048]{1,0:T(8,128)}, u32[]{:S(2)}, u32[]{:S(2)}) collective-permute-start(f32[128,2048]{1,0:T(8,128)S(1)} %copy-done.95), channel_id=1, source_target_pairs={{0,1},{3,2},{4,5},{7,6},{8,9},{11,10},{12,13},{15,14},{16,17},{19,... | collective-permute-start | bytes 3145736 | tf_op jit(solution)/shard_map/ppermute | solution.py:619
  441.7 23.8 %all-reduce.5 = (f32[2048]{0:T(1024)}, f32[2048]{0:T(1024)}, f32[8,1024]{1,0:T(8,128)S(1)}, f32[8,16]{1,0:T(8,128)S(1)}) all-reduce(f32[2048]{0:T(1024)S(1)} %bitcast.103, f32[2048]{0:T(1024)S(1)} %bitcast.102, f32[8,1024]{1,0:T(8,128)S(1)} %copy-done.118, f32[8,16]{1,0:T(8,128)S(1)} %copy-done.124), channel_id=1, replica_groups=mesh['dp'=8,'tensor'=4] {'dp'}, use_global_device_ids=true, to_apply=%region_8.9 | all-reduce | flops 12416 | bytes 99328 | tf_op jit(solution)/shard_map/psum | solution.py:775
  467.4 7.1 %collective-permute-done.15 = f32[256,2048]{1,0:T(8,128)} collective-permute-done((f32[256,2048]{1,0:T(8,128)}, f32[256,2048]{1,0:T(8,128)}, u32[]{:S(2)}, u32[]{:S(2)}) %collective-permute-start.15) | collective-permute-done | bytes 2097184 | tf_op jit(solution)/shard_map/ppermute | solution.py:619
  481.0 6.8 %fusion.95 = f32[2048,1024]{1,0:T(8,128)} fusion(bf16[1024,1024]{1,0:T(8,128)(2,1)S(1)} %copy-done.96, bf16[256,2048]{1,0:T(8,128)(2,1)S(1)} %copy-done.87, bf16[256,2048]{1,0:T(8,128)(2,1)S(1)} %copy-done.90, bf16[256,2048]{1,0:T(8,128)(2,1)S(1)} %copy-done.93, bf16[256,2048]{1,0:T(8,128)(2,1)S(1)} %copy-done.84), kind=kOutput, calls=%fused_computation.181 | convolution fusion | flops 4311744512 | bytes 14680064 | tf_op jit(solution)/shard_map/dot_general | solution.py:25
  503.6 8.8 %collective-permute-done.16 = f32[128,2048]{1,0:T(8,128)S(1)} collective-permute-done((f32[128,2048]{1,0:T(8,128)}, f32[128,2048]{1,0:T(8,128)S(1)}, u32[]{:S(2)}, u32[]{:S(2)}) %collective-permute-start.16) | collective-permute-done | bytes 1048608 | tf_op jit(solution)/shard_map/ppermute | solution.py:619
  512.3 21.8 %collective-permute-done.19 = f32[256,2048]{1,0:T(8,128)S(1)} collective-permute-done((f32[256,2048]{1,0:T(8,128)}, f32[256,2048]{1,0:T(8,128)S(1)}, u32[]{:S(2)}, u32[]{:S(2)}) %collective-permute-start.19) | collective-permute-done | bytes 2097184 | tf_op jit(solution)/shard_map/ppermute | solution.py:619
  572.3 14.0 %collective-permute-done.24 = f32[40,2048]{1,0:T(8,128)S(1)} collective-permute-done((f32[40,2048]{1,0:T(8,128)S(1)}, f32[40,2048]{1,0:T(8,128)S(1)}, u32[]{:S(2)}, u32[]{:S(2)}) %collective-permute-start.24) | collective-permute-done | bytes 327712 | tf_op jit(solution)/shard_map/ppermute | solution.py:619
  (447 shorter events, 229.9 us)
Async XLA Ops:
  7.2 342.3 %reduce-scatter.5.cloned.1.call-start = ((), (), s32[]{:S(2)}) async-start(), calls=%async_computation.4 | async-start | bytes 9437184 | tf_op jit(solution)/shard_map/reduce_scatter | solution.py:764
  7.9 106.4 %copy-start.35 = (f32[1024]{0:T(1024)}, f32[1024]{0:T(1024)S(1)}, u32[]{:S(2)}) copy-start(f32[1024]{0:T(1024)S(1)} %convert_element_type.120) | copy-start | bytes 12292
  13.8 100.6 %copy-start.21 = (bf16[16,1024]{1,0:T(8,128)(2,1)}, bf16[16,1024]{1,0:T(8,128)(2,1)S(1)}, u32[]{:S(2)}) copy-start(bf16[16,1024]{1,0:T(8,128)(2,1)S(1)} %fusion.53.spread_ref) | copy-start | bytes 98308
  14.5 99.8 %copy-start.1 = (f32[1024,16]{1,0:T(8,128)}, f32[1024,16]{1,0:T(8,128)S(1)}, u32[]{:S(2)}) copy-start(f32[1024,16]{1,0:T(8,128)S(1)} %copy.109.aux_ref) | copy-start | bytes 196612
  37.6 58.8 %collective-permute-start = (f32[256,2048]{1,0:T(8,128)}, f32[256,2048]{1,0:T(8,128)}, u32[]{:S(2)}, u32[]{:S(2)}) collective-permute-start(f32[256,2048]{1,0:T(8,128)} %fusion.106), channel_id=1, source_target_pairs={{0,1},{3,2},{4,5},{7,6},{8,9},{11,10},{12,13},{15,14},{16,17},{19,... | collective-permute-start | bytes 6291464 | tf_op jit(solution)/shard_map/ppermute | solution.py:619
  100.7 54.6 %collective-permute-start.2 = (f32[256,2048]{1,0:T(8,128)}, f32[256,2048]{1,0:T(8,128)}, u32[]{:S(2)}, u32[]{:S(2)}) collective-permute-start(f32[256,2048]{1,0:T(8,128)} %add.230), channel_id=1, source_target_pairs={{1,2},{2,1},{5,6},{6,5},{9,10},{10,9},{13,14},{14,13},{17,18},{18,... | collective-permute-start | bytes 6291464 | tf_op jit(solution)/shard_map/ppermute | solution.py:619
  102.6 52.7 %collective-permute-start.1 = (f32[256,2048]{1,0:T(8,128)}, f32[256,2048]{1,0:T(8,128)}, u32[]{:S(2)}, u32[]{:S(2)}) collective-permute-start(f32[256,2048]{1,0:T(8,128)} %fusion.114), channel_id=1, source_target_pairs={{0,1},{3,2},{4,5},{7,6},{8,9},{11,10},{12,13},{15,14},{16,17},{19,... | collective-permute-start | bytes 6291464 | tf_op jit(solution)/shard_map/ppermute | solution.py:619
  163.5 42.9 %collective-permute-start.4 = (f32[256,2048]{1,0:T(8,128)}, f32[256,2048]{1,0:T(8,128)}, u32[]{:S(2)}, u32[]{:S(2)}) collective-permute-start(f32[256,2048]{1,0:T(8,128)} %add.233), channel_id=1, source_target_pairs={{1,2},{2,1},{5,6},{6,5},{9,10},{10,9},{13,14},{14,13},{17,18},{18,... | collective-permute-start | bytes 6291464 | tf_op jit(solution)/shard_map/ppermute | solution.py:619
  165.7 45.3 %collective-permute-start.3 = (f32[256,2048]{1,0:T(8,128)}, f32[256,2048]{1,0:T(8,128)S(1)}, u32[]{:S(2)}, u32[]{:S(2)}) collective-permute-start(f32[256,2048]{1,0:T(8,128)} %add_select_fusion.4), channel_id=1, source_target_pairs={{0,1},{3,2},{1,0},{2,3},{4,5},{7,6},{5,4},{6,7},{8,9},{11,10},{9,8... | collective-permute-start | bytes 6291464 | tf_op jit(solution)/shard_map/ppermute | solution.py:619
  219.1 200.3 %reduce-scatter.7.cloned.1.call-start = ((), (), s32[]{:S(2)}) async-start(), calls=%async_computation.5 | async-start | bytes 3538944 | tf_op jit(solution)/shard_map/reduce_scatter | solution.py:772
  219.2 30.6 %collective-permute-start.6 = (f32[256,2048]{1,0:T(8,128)}, f32[256,2048]{1,0:T(8,128)S(1)}, u32[]{:S(2)}, u32[]{:S(2)}) collective-permute-start(f32[256,2048]{1,0:T(8,128)} %add.237), channel_id=1, source_target_pairs={{1,2},{2,1},{5,6},{6,5},{9,10},{10,9},{13,14},{14,13},{17,18},{18,... | collective-permute-start | bytes 6291464 | tf_op jit(solution)/shard_map/ppermute | solution.py:619
  220.2 46.0 %collective-permute-start.5 = (f32[256,2048]{1,0:T(8,128)}, f32[256,2048]{1,0:T(8,128)S(1)}, u32[]{:S(2)}, u32[]{:S(2)}) collective-permute-start(f32[256,2048]{1,0:T(8,128)} %add_select_fusion.3), channel_id=1, source_target_pairs={{0,1},{3,2},{1,0},{2,3},{4,5},{7,6},{5,4},{6,7},{8,9},{11,10},{9,8... | collective-permute-start | bytes 6291464 | tf_op jit(solution)/shard_map/ppermute | solution.py:619
  272.1 29.9 %collective-permute-start.8 = (f32[256,2048]{1,0:T(8,128)}, f32[256,2048]{1,0:T(8,128)}, u32[]{:S(2)}, u32[]{:S(2)}) collective-permute-start(f32[256,2048]{1,0:T(8,128)} %add.240), channel_id=1, source_target_pairs={{1,2},{2,1},{5,6},{6,5},{9,10},{10,9},{13,14},{14,13},{17,18},{18,... | collective-permute-start | bytes 6291464 | tf_op jit(solution)/shard_map/ppermute | solution.py:619
  274.5 43.7 %collective-permute-start.7 = (f32[256,2048]{1,0:T(8,128)S(1)}, f32[256,2048]{1,0:T(8,128)S(1)}, u32[]{:S(2)}, u32[]{:S(2)}) collective-permute-start(f32[256,2048]{1,0:T(8,128)S(1)} %add_select_fusion.2), channel_id=1, source_target_pairs={{0,1},{3,2},{1,0},{2,3},{4,5},{7,6},{5,4},{6,7},{8,9},{11,10},{9,8... | collective-permute-start | bytes 6291464 | tf_op jit(solution)/shard_map/ppermute | solution.py:619
  325.5 41.2 %collective-permute-start.10 = (f32[256,2048]{1,0:T(8,128)}, f32[256,2048]{1,0:T(8,128)}, u32[]{:S(2)}, u32[]{:S(2)}) collective-permute-start(f32[256,2048]{1,0:T(8,128)} %add.243), channel_id=1, source_target_pairs={{1,2},{2,1},{5,6},{6,5},{9,10},{10,9},{13,14},{14,13},{17,18},{18,... | collective-permute-start | bytes 6291464 | tf_op jit(solution)/shard_map/ppermute | solution.py:619
  327.6 42.9 %collective-permute-start.9 = (f32[256,2048]{1,0:T(8,128)}, f32[256,2048]{1,0:T(8,128)S(1)}, u32[]{:S(2)}, u32[]{:S(2)}) collective-permute-start(f32[256,2048]{1,0:T(8,128)} %add_select_fusion.1), channel_id=1, source_target_pairs={{0,1},{3,2},{1,0},{2,3},{4,5},{7,6},{5,4},{6,7},{8,9},{11,10},{9,8... | collective-permute-start | bytes 6291464 | tf_op jit(solution)/shard_map/ppermute | solution.py:619
  355.6 237.4 %reduce-scatter.9.cloned.1.call-start = ((), (), s32[]{:S(2)}) async-start(), calls=%async_computation.6 | async-start | bytes 9437184 | tf_op jit(solution)/shard_map/reduce_scatter | solution.py:774
  378.0 41.5 %collective-permute-start.11 = (f32[256,2048]{1,0:T(8,128)}, f32[256,2048]{1,0:T(8,128)S(1)}, u32[]{:S(2)}, u32[]{:S(2)}) collective-permute-start(f32[256,2048]{1,0:T(8,128)} %add_select_fusion), channel_id=1, source_target_pairs={{0,1},{3,2},{1,0},{2,3},{4,5},{7,6},{5,4},{6,7},{8,9},{11,10},{9,8... | collective-permute-start | bytes 6291464 | tf_op jit(solution)/shard_map/ppermute | solution.py:619
  379.7 39.7 %collective-permute-start.12 = (f32[256,2048]{1,0:T(8,128)}, f32[256,2048]{1,0:T(8,128)}, u32[]{:S(2)}, u32[]{:S(2)}) collective-permute-start(f32[256,2048]{1,0:T(8,128)} %add.246), channel_id=1, source_target_pairs={{1,2},{2,1},{5,6},{6,5},{9,10},{10,9},{13,14},{14,13},{17,18},{18,... | collective-permute-start | bytes 6291464 | tf_op jit(solution)/shard_map/ppermute | solution.py:619
  426.5 166.5 %reduce-scatter.11.cloned.1.call-start = ((), (), s32[]{:S(2)}) async-start(), calls=%async_computation.7 | async-start | bytes 9437184 | tf_op jit(solution)/shard_map/reduce_scatter | solution.py:784
  426.6 40.8 %collective-permute-start.14 = (f32[256,2048]{1,0:T(8,128)}, f32[256,2048]{1,0:T(8,128)}, u32[]{:S(2)}, u32[]{:S(2)}) collective-permute-start(f32[256,2048]{1,0:T(8,128)} %add.247), channel_id=1, source_target_pairs={{1,2},{2,1},{5,6},{6,5},{9,10},{10,9},{13,14},{14,13},{17,18},{18,... | collective-permute-start | bytes 6291464 | tf_op jit(solution)/shard_map/ppermute | solution.py:619
  428.7 45.8 %collective-permute-start.15 = (f32[256,2048]{1,0:T(8,128)}, f32[256,2048]{1,0:T(8,128)}, u32[]{:S(2)}, u32[]{:S(2)}) collective-permute-start(f32[256,2048]{1,0:T(8,128)} %add.248), channel_id=1, source_target_pairs={{1,0},{2,3},{5,4},{6,7},{9,8},{10,11},{13,12},{14,15},{17,16},{18,... | collective-permute-start | bytes 6291464 | tf_op jit(solution)/shard_map/ppermute | solution.py:619
  431.8 35.5 %collective-permute-start.13 = (f32[128,2048]{1,0:T(8,128)S(1)}, f32[128,2048]{1,0:T(8,128)}, u32[]{:S(2)}, u32[]{:S(2)}) collective-permute-start(f32[128,2048]{1,0:T(8,128)S(1)} %copy-done.95), channel_id=1, source_target_pairs={{0,1},{3,2},{4,5},{7,6},{8,9},{11,10},{12,13},{15,14},{16,17},{19,... | collective-permute-start | bytes 3145736 | tf_op jit(solution)/shard_map/ppermute | solution.py:619
  488.8 14.8 %collective-permute-start.17 = (f32[40,2048]{1,0:T(8,128)S(1)}, f32[40,2048]{1,0:T(8,128)S(1)}, u32[]{:S(2)}, u32[]{:S(2)}) collective-permute-start(f32[40,2048]{1,0:T(8,128)S(1)} %copy-done.108), channel_id=1, source_target_pairs={{0,1},{3,2},{4,5},{7,6},{8,9},{11,10},{12,13},{15,14},{16,17},{19,... | collective-permute-start | bytes 983048 | tf_op jit(solution)/shard_map/ppermute | solution.py:619
  490.2 22.1 %collective-permute-start.16 = (f32[128,2048]{1,0:T(8,128)}, f32[128,2048]{1,0:T(8,128)S(1)}, u32[]{:S(2)}, u32[]{:S(2)}) collective-permute-start(f32[128,2048]{1,0:T(8,128)} %get-tuple-element.386), channel_id=1, source_target_pairs={{0,1},{3,2},{4,5},{7,6},{8,9},{11,10},{12,13},{15,14},{16,17},{19,... | collective-permute-start | bytes 3145736 | tf_op jit(solution)/shard_map/ppermute | solution.py:619
  491.6 20.7 %collective-permute-start.18 = (f32[128,2048]{1,0:T(8,128)S(1)}, f32[128,2048]{1,0:T(8,128)S(1)}, u32[]{:S(2)}, u32[]{:S(2)}) collective-permute-start(f32[128,2048]{1,0:T(8,128)S(1)} %add.249), channel_id=1, source_target_pairs={{1,2},{2,1},{5,6},{6,5},{9,10},{10,9},{13,14},{14,13},{17,18},{18,... | collective-permute-start | bytes 3145736 | tf_op jit(solution)/shard_map/ppermute | solution.py:619
  492.3 41.8 %collective-permute-start.19 = (f32[256,2048]{1,0:T(8,128)}, f32[256,2048]{1,0:T(8,128)S(1)}, u32[]{:S(2)}, u32[]{:S(2)}) collective-permute-start(f32[256,2048]{1,0:T(8,128)} %add.250), channel_id=1, source_target_pairs={{1,0},{2,3},{5,4},{6,7},{9,8},{10,11},{13,12},{14,15},{17,16},{18,... | collective-permute-start | bytes 6291464 | tf_op jit(solution)/shard_map/ppermute | solution.py:619
  536.1 17.7 %collective-permute-start.21 = (f32[40,2048]{1,0:T(8,128)}, f32[40,2048]{1,0:T(8,128)S(1)}, u32[]{:S(2)}, u32[]{:S(2)}) collective-permute-start(f32[40,2048]{1,0:T(8,128)} %add.256), channel_id=1, source_target_pairs={{1,2},{2,1},{5,6},{6,5},{9,10},{10,9},{13,14},{14,13},{17,18},{18,... | collective-permute-start | bytes 983048 | tf_op jit(solution)/shard_map/ppermute | solution.py:619
  536.8 17.0 %collective-permute-start.20 = (f32[128,2048]{1,0:T(8,128)}, f32[128,2048]{1,0:T(8,128)}, u32[]{:S(2)}, u32[]{:S(2)}) collective-permute-start(f32[128,2048]{1,0:T(8,128)} %add.255), channel_id=1, source_target_pairs={{1,2},{2,1},{5,6},{6,5},{9,10},{10,9},{13,14},{14,13},{17,18},{18,... | collective-permute-start | bytes 3145736 | tf_op jit(solution)/shard_map/ppermute | solution.py:619
  538.5 18.8 %collective-permute-start.22 = (f32[128,2048]{1,0:T(8,128)S(1)}, f32[128,2048]{1,0:T(8,128)}, u32[]{:S(2)}, u32[]{:S(2)}) collective-permute-start(f32[128,2048]{1,0:T(8,128)S(1)} %add.257), channel_id=1, source_target_pairs={{1,0},{2,3},{5,4},{6,7},{9,8},{10,11},{13,12},{14,15},{17,16},{18,... | collective-permute-start | bytes 3145736 | tf_op jit(solution)/shard_map/ppermute | solution.py:619
  560.1 26.3 %collective-permute-start.23 = (f32[128,2048]{1,0:T(8,128)S(1)}, f32[128,2048]{1,0:T(8,128)S(1)}, u32[]{:S(2)}, u32[]{:S(2)}) collective-permute-start(f32[128,2048]{1,0:T(8,128)S(1)} %add.261), channel_id=1, source_target_pairs={{1,0},{2,3},{5,4},{6,7},{9,8},{10,11},{13,12},{14,15},{17,16},{18,... | collective-permute-start | bytes 3145736 | tf_op jit(solution)/shard_map/ppermute | solution.py:619
  566.3 20.1 %collective-permute-start.24 = (f32[40,2048]{1,0:T(8,128)S(1)}, f32[40,2048]{1,0:T(8,128)S(1)}, u32[]{:S(2)}, u32[]{:S(2)}) collective-permute-start(f32[40,2048]{1,0:T(8,128)S(1)} %add.262), channel_id=1, source_target_pairs={{1,0},{2,3},{5,4},{6,7},{9,8},{10,11},{13,12},{14,15},{17,16},{18,... | collective-permute-start | bytes 983048 | tf_op jit(solution)/shard_map/ppermute | solution.py:619
  (129 other events, 1134.3 us)
Sparse Core Ops, SparseCore 0:
  219.3 70.8 reduce-scatter.4
  355.7 45.7 reduce-scatter.6
  426.7 74.1 reduce-scatter.8
  505.2 71.2 reduce-scatter.10
